TPU v7x, 512 devices: a whole 4x8x8 slice. The times are simulated.
512 devices in a mesh: shot: 32 (over y, z_lo), depth: 16 (over z_hi, x, core).
Axes of the slice: x: 4, y: 8, z: 8 (z_hi: 2, z_lo: 4; z = z_hi * 4 + z_lo), core: 2. Of those that a mesh axis runs over, the one named last changes fastest.
Arguments:
- courant_sq: float32 [128, 64, 128], P('depth'), may hold values from 0.03 to 0.245
- momentum: float32 [128, 64, 128], P('depth'), may hold values from -6 to 6
- fwd_prev: float32 [64, 128, 64, 128], P('shot', 'depth'), may hold values from -6 to 6
- fwd_cur: float32 [64, 128, 64, 128], P('shot', 'depth'), may hold values from -6 to 6
- adj_next: float32 [64, 128, 64, 128], P('shot', 'depth'), may hold values from -6 to 6
- adj_cur: float32 [64, 128, 64, 128], P('shot', 'depth'), may hold values from -6 to 6
- observed: float32 [64, 8, 512], P('shot'), may hold values from -24 to 24
- src_cells: int32 [64], P('shot'), may hold values from 0 to 1048575
- rec_cells: int32 [64, 512], P('shot'), may hold values from 0 to 1048575
- ckpt_step: int32 [], replicated, may hold values from 0 to 999999
Outputs:
- momentum_half: float32 [128, 64, 128], P('depth')
- kinetic: float32 [], replicated
All inputs are finite; a program needn't handle non-finite values.
Results may differ from a plain program's by a relative error of at most 0.0003.
Values sent between devices are 32-bit elements; how exact they have to be, the bound alone decides.
A program may use at most 64 MiB of HBM per device.

v0:
```python
import jax
import jax.numpy as jnp
from jax import lax
from jax.sharding import PartitionSpec as P

CENTER = -2.5
NEAR = 4.0 / 3.0
FAR = -1.0 / 12.0
AMPLITUDE = 100.0
EPSILON = 1e-06


def with_halo(value, sides, width):
    for axis, dim in sides:
        size, length = (lax.axis_size(axis), value.shape[dim])
        up = [(i, (i + 1) % size) for i in range(size - 1)]
        down = [(j, i) for i, j in up]
        last = lax.slice_in_dim(value, length - width, length, axis=dim)
        leading = lax.slice_in_dim(value, 0, width, axis=dim)
        before = lax.ppermute(last, axis, up)
        after = lax.ppermute(leading, axis, down)
        value = jnp.concatenate([before, value, after], axis=dim)
    return value


def laplace(padded):
    lateral = jnp.pad(padded[:, 2:-2], ((0, 0), (0, 0), (2, 2), (2, 2)))
    center = padded[:, 2:-2]
    along_z = NEAR * (padded[:, 1:-3] + padded[:, 3:-1]) + FAR * (padded[:, :-4] + padded[:, 4:])
    along_x = NEAR * (lateral[:, :, 1:-3, 2:-2] + lateral[:, :, 3:-1, 2:-2]) + FAR * (
        lateral[:, :, :-4, 2:-2] + lateral[:, :, 4:, 2:-2]
    )
    along_y = NEAR * (lateral[:, :, 2:-2, 1:-3] + lateral[:, :, 2:-2, 3:-1]) + FAR * (
        lateral[:, :, 2:-2, :-4] + lateral[:, :, 2:-2, 4:]
    )
    return 3.0 * CENTER * center + along_z + along_x + along_y


def locate(field, cell_ids, first_plane):
    shot_count, planes, rows_x, rows_y = field.shape
    plane_cells = rows_x * rows_y
    local_index = cell_ids - first_plane * plane_cells
    inside = (local_index >= 0) & (local_index < planes * plane_cells)
    target = jnp.where(inside, local_index, 0)
    return (inside, target)


def inject(field, cell_ids, values, first_plane):
    shot_count = field.shape[0]
    inside, target = locate(field, cell_ids, first_plane)
    amount = jnp.where(inside, values, jnp.zeros_like(values))
    flattened = field.reshape(shot_count, -1)
    lanes = jnp.arange(shot_count)[:, None]
    flattened = flattened.at[lanes, target].add(amount)
    return flattened.reshape(field.shape)


def sample(field, cell_ids, first_plane):
    shot_count = field.shape[0]
    inside, target = locate(field, cell_ids, first_plane)
    values = jnp.take_along_axis(field.reshape(shot_count, -1), target, axis=1)
    return jnp.where(inside, values, jnp.zeros_like(values))


def wave_value(start, step):
    cycle = jnp.mod(start + jnp.int32(step), jnp.int32(48))
    phase = (cycle.astype(jnp.float32) - 24.0) / 12.0
    return AMPLITUDE * (1.0 - 2.0 * phase * phase) * jnp.exp(-phase * phase)


def statistics(scaled, moment, weight, cells_all):
    grand_total = lax.psum(jnp.sum(scaled * scaled), ("shot", "depth"))
    factor = lax.rsqrt(grand_total / cells_all + EPSILON)
    halfway = moment - 0.5 * factor * scaled
    energy = lax.psum(jnp.sum(weight * halfway * halfway), ("shot", "depth"))
    return (factor, 0.5 * energy / cells_all)


def shards(
    courant_sq,
    momentum,
    fwd_prev,
    fwd_cur,
    adj_next,
    adj_cur,
    observed,
    src_cells,
    rec_cells,
    ckpt_step,
):
    shot_count, planes, rows_x, rows_y = fwd_cur.shape
    steps_all = observed.shape[1]
    first_plane = lax.axis_index("depth") * planes
    total_planes = planes * lax.axis_size("depth")
    cells_all = total_planes * rows_x * rows_y
    sources = src_cells[:, None]
    older, current = (fwd_prev, fwd_cur)
    laplacians = []
    misfits = []
    for step in range(steps_all):
        padded = with_halo(current, (("depth", 1),), 2)
        strength = jnp.full(sources.shape, wave_value(ckpt_step, step), jnp.float32)
        laplacian = inject(laplace(padded), sources, strength, first_plane)
        newer = 2.0 * current - older + courant_sq * laplacian
        misfits.append(sample(newer, rec_cells, first_plane) - observed[:, step, :])
        laplacians.append(laplacian)
        older, current = (current, newer)
    adj_later, adj_now = (adj_next, adj_cur)
    gradient = jnp.zeros((planes, rows_x, rows_y), jnp.float32)
    for step in reversed(range(steps_all)):
        padded = with_halo(courant_sq * adj_now, (("depth", 1),), 2)
        adj_new = 2.0 * adj_now - adj_later + laplace(padded)
        adj_new = inject(adj_new, rec_cells, misfits[step], first_plane)
        gradient = gradient + jnp.sum(adj_new * laplacians[step], axis=0)
        adj_later, adj_now = (adj_now, adj_new)
    depths = (first_plane + jnp.arange(planes)).astype(jnp.float32)
    weight = (1.0 + 2.0 * depths / (total_planes - 1))[:, None, None]
    share_rows = rows_x // lax.axis_size("shot")
    offset = lax.axis_index("shot") * share_rows
    moment_share = lax.dynamic_slice_in_dim(momentum, offset, share_rows, 1)
    gradient = lax.psum(gradient, "shot")
    scaled = weight * gradient
    scaled_share = lax.dynamic_slice_in_dim(scaled, offset, share_rows, 1)
    factor, kinetic = statistics(scaled_share, moment_share, weight, cells_all)
    momentum_half = momentum - 0.5 * factor * scaled
    return (momentum_half, kinetic)


def solution(mesh):
    placed = (
        P("depth", None, None),
        P("depth", None, None),
        P("shot", "depth", None, None),
        P("shot", "depth", None, None),
        P("shot", "depth", None, None),
        P("shot", "depth", None, None),
        P("shot", None, None),
        P("shot"),
        P("shot", None),
        P(),
    )
    return jax.shard_map(
        shards, mesh=mesh, in_specs=placed, out_specs=(P("depth", None, None), P()), check_vma=False
    )
```

profile of v0, /device:TPU:1, one launch (start us, length us, event | category | flops | bytes accessed | tf_op | source)
XLA Modules:
  0.0 933.5 jit_solution(2792217980189953025)
XLA Ops:
  8.3 4.5 collective-permute-start.2
  12.8 5.6 collective-permute-start.3
  25.2 2.4 collective-permute-start.5
  27.7 3.9 collective-permute-done.5
  38.5 3.9 collective-permute-done.7
  49.3 15.6 %collective-permute-done.9 = f32[2,2,64,128]{3,2,1,0:T(8,128)S(1)} collective-permute-done((f32[2,2,64,128]{3,2,1,0:T(8,128)S(1)}, f32[2,2,64,128]{3,2,1,0:T(8,128)S(1)}, u32[]{:S(2)}, u32[]{:S(2)}) %collective-permute-start.9) | collective-permute-done | bytes 131104 | tf_op jit(solution)/shard_map/ppermute | solution.py:21
  69.4 2.4 collective-permute-start.11
  72.0 10.3 %collective-permute-done.11 = f32[2,2,64,128]{3,2,1,0:T(8,128)S(1)} collective-permute-done((f32[2,2,64,128]{3,2,1,0:T(8,128)S(1)}, f32[2,2,64,128]{3,2,1,0:T(8,128)S(1)}, u32[]{:S(2)}, u32[]{:S(2)}) %collective-permute-start.11) | collective-permute-done | bytes 131104 | tf_op jit(solution)/shard_map/ppermute | solution.py:21
  89.3 9.3 collective-permute-done.13
  103.6 2.6 collective-permute-start.15
  106.7 9.1 gather_fusion.7
  121.6 9.1 collective-permute-start.16
  133.0 9.1 gather_fusion.6
  142.6 9.1 gather_fusion.5
  152.1 9.1 gather_fusion.4
  161.7 9.1 gather_fusion.3
  171.2 9.1 gather_fusion.2
  180.8 9.1 gather_fusion.1
  194.1 9.1 gather_fusion
  203.3 3.8 collective-permute-start
  209.6 7.4 collective-permute-done.1
  217.7 7.7 scatter_fusion.8
  227.4 2.4 collective-permute-start.19
  229.9 9.9 %collective-permute-done.19 = f32[2,2,64,128]{3,2,1,0:T(8,128)S(1)} collective-permute-done((f32[2,2,64,128]{3,2,1,0:T(8,128)S(1)}, f32[2,2,64,128]{3,2,1,0:T(8,128)S(1)}, u32[]{:S(2)}, u32[]{:S(2)}) %collective-permute-start.19) | collective-permute-done | bytes 131104 | tf_op jit(solution)/shard_map/ppermute | solution.py:21
  240.4 7.5 scatter_fusion.9
  252.3 9.9 %collective-permute-done.21 = f32[2,2,64,128]{3,2,1,0:T(8,128)S(1)} collective-permute-done((f32[2,2,64,128]{3,2,1,0:T(8,128)S(1)}, f32[2,2,64,128]{3,2,1,0:T(8,128)S(1)}, u32[]{:S(2)}, u32[]{:S(2)}) %collective-permute-start.21) | collective-permute-done | bytes 131104 | tf_op jit(solution)/shard_map/ppermute | solution.py:21
  262.8 7.5 scatter_fusion.10
  270.4 4.1 collective-permute-start.22
  276.4 16.3 %collective-permute-done.23 = f32[2,2,64,128]{3,2,1,0:T(8,128)S(1)} collective-permute-done((f32[2,2,64,128]{3,2,1,0:T(8,128)S(1)}, f32[2,2,64,128]{3,2,1,0:T(8,128)S(1)}, u32[]{:S(2)}, u32[]{:S(2)}) %collective-permute-start.23) | collective-permute-done | bytes 131104 | tf_op jit(solution)/shard_map/ppermute | solution.py:21
  293.3 7.5 scatter_fusion.11
  303.5 2.4 collective-permute-start.25
  308.1 7.8 collective-permute-done.25
  317.5 7.6 scatter_fusion.12
  327.8 2.8 collective-permute-start.27
  330.7 3.4 multiply_reduce_fusion.6
  336.3 4.2 collective-permute-done.27
  342.1 7.5 scatter_fusion.13
  350.4 4.9 collective-permute-start.28
  357.3 2.7 multiply_reduce_fusion.4
  361.5 3.4 collective-permute-done.29
  366.5 7.5 scatter_fusion.14
  374.8 3.2 collective-permute-start.30
  380.1 2.7 multiply_reduce_fusion.2
  383.1 5.9 collective-permute-done.31
  389.6 7.5 scatter_fusion.15
  401.3 308.0 %all-reduce.18.cloned.1.call-done = f32[8,64,128]{2,1,0:T(8,128)} async-done(((f32[8,64,128]{2,1,0:T(8,128)}), f32[8,64,128]{2,1,0:T(8,128)}) %all-reduce.18.cloned.1.call-update) | async-done | bytes 262160 | tf_op jit(solution)/shard_map/psum | solution.py:121
  711.1 116.8 %psum.22 = f32[]{:T(128)} all-reduce(f32[]{:T(128)} %multiply_reduce_fusion.9), channel_id=1, replica_groups=mesh['shot'=32,'depth'=16] {'shot','depth'}, use_global_device_ids=true, to_apply=%region_26.28 | all-reduce | flops 1 | bytes 8 | tf_op jit(solution)/shard_map/psum | solution.py:72
  829.3 94.6 %psum.23 = f32[]{:T(128)} all-reduce(f32[]{:T(128)} %fusion.324), channel_id=1, replica_groups=mesh['shot'=32,'depth'=16] {'shot','depth'}, use_global_device_ids=true, to_apply=%region_28.30 | all-reduce | flops 1 | bytes 8 | tf_op jit(solution)/shard_map/psum | solution.py:75
  (260 shorter events, 95.0 us)
Async XLA Ops:
  7.2 12.8 %copy-start.7 = (f32[2,8,64,128]{3,2,1,0:T(8,128)S(1)}, f32[2,8,64,128]{3,2,1,0:T(8,128)}, u32[]{:S(2)}) copy-start(f32[2,8,64,128]{3,2,1,0:T(8,128)} %param.15) | copy-start | bytes 1572868
  7.2 12.4 %copy-start.42 = (s32[2]{0:T(128)S(1)}, s32[2]{0:T(128)}, u32[]{:S(2)}) copy-start(s32[2]{0:T(128)} %param.19) | copy-start | bytes 28
  7.2 702.2 %all-reduce.18.cloned.1.call-start = ((), (), s32[]{:S(2)}) async-start(), calls=%async_computation | async-start | bytes 524288 | tf_op jit(solution)/shard_map/psum | solution.py:121
  8.3 11.7 %collective-permute-start.2 = (f32[2,2,64,128]{3,2,1,0:T(8,128)S(1)}, f32[2,2,64,128]{3,2,1,0:T(8,128)S(1)}, u32[]{:S(2)}, u32[]{:S(2)}) collective-permute-start(f32[2,2,64,128]{3,2,1,0:T(8,128)S(1)} %get-tuple-element.40), channel_id=1, source_target_pairs={{0,1},{1,2},{2,3},{3,4},{4,5},{5,6},{6,7},{7,8},{8,9},{9,10},{10,1... | collective-permute-start | bytes 393224 | tf_op jit(solution)/shard_map/ppermute | solution.py:20
  12.8 7.3 collective-permute-start.3
  23.3 4.3 collective-permute-start.4
  25.2 6.3 collective-permute-start.5
  34.2 4.3 collective-permute-start.6
  36.1 6.3 collective-permute-start.7
  44.9 4.4 collective-permute-start.8
  47.1 17.8 %collective-permute-start.9 = (f32[2,2,64,128]{3,2,1,0:T(8,128)S(1)}, f32[2,2,64,128]{3,2,1,0:T(8,128)S(1)}, u32[]{:S(2)}, u32[]{:S(2)}) collective-permute-start(f32[2,2,64,128]{3,2,1,0:T(8,128)S(1)} %get-tuple-element.33), channel_id=1, source_target_pairs={{1,0},{2,1},{3,2},{4,3},{5,4},{6,5},{7,6},{8,7},{9,8},{10,9},{11,1... | collective-permute-start | bytes 393224 | tf_op jit(solution)/shard_map/ppermute | solution.py:21
  67.4 4.5 collective-permute-start.10
  69.4 12.9 %collective-permute-start.11 = (f32[2,2,64,128]{3,2,1,0:T(8,128)S(1)}, f32[2,2,64,128]{3,2,1,0:T(8,128)S(1)}, u32[]{:S(2)}, u32[]{:S(2)}) collective-permute-start(f32[2,2,64,128]{3,2,1,0:T(8,128)S(1)} %get-tuple-element.31), channel_id=1, source_target_pairs={{1,0},{2,1},{3,2},{4,3},{5,4},{6,5},{7,6},{8,7},{9,8},{10,9},{11,1... | collective-permute-start | bytes 393224 | tf_op jit(solution)/shard_map/ppermute | solution.py:21
  84.9 14.3 %copy-start.3 = (f32[2,8,64,128]{3,2,1,0:T(8,128)}, f32[2,8,64,128]{3,2,1,0:T(8,128)S(1)}, u32[]{:S(2)}) copy-start(f32[2,8,64,128]{3,2,1,0:T(8,128)S(1)} %multiply_add_fusion.3) | copy-start | bytes 1572868
  84.9 4.4 collective-permute-start.12
  86.9 11.7 %collective-permute-start.13 = (f32[2,2,64,128]{3,2,1,0:T(8,128)S(1)}, f32[2,2,64,128]{3,2,1,0:T(8,128)S(1)}, u32[]{:S(2)}, u32[]{:S(2)}) collective-permute-start(f32[2,2,64,128]{3,2,1,0:T(8,128)S(1)} %get-tuple-element.29), channel_id=1, source_target_pairs={{1,0},{2,1},{3,2},{4,3},{5,4},{6,5},{7,6},{8,7},{9,8},{10,9},{11,1... | collective-permute-start | bytes 393224 | tf_op jit(solution)/shard_map/ppermute | solution.py:21
  101.7 14.1 %collective-permute-start.14 = (f32[2,2,64,128]{3,2,1,0:T(8,128)S(1)}, f32[2,2,64,128]{3,2,1,0:T(8,128)S(1)}, u32[]{:S(2)}, u32[]{:S(2)}) collective-permute-start(f32[2,2,64,128]{3,2,1,0:T(8,128)S(1)} %get-tuple-element.26), channel_id=1, source_target_pairs={{0,1},{1,2},{2,3},{3,4},{4,5},{5,6},{6,7},{7,8},{8,9},{9,10},{10,1... | collective-permute-start | bytes 393224 | tf_op jit(solution)/shard_map/ppermute | solution.py:20
  103.6 12.9 %collective-permute-start.15 = (f32[2,2,64,128]{3,2,1,0:T(8,128)S(1)}, f32[2,2,64,128]{3,2,1,0:T(8,128)S(1)}, u32[]{:S(2)}, u32[]{:S(2)}) collective-permute-start(f32[2,2,64,128]{3,2,1,0:T(8,128)S(1)} %get-tuple-element.27), channel_id=1, source_target_pairs={{1,0},{2,1},{3,2},{4,3},{5,4},{6,5},{7,6},{8,7},{9,8},{10,9},{11,1... | collective-permute-start | bytes 393224 | tf_op jit(solution)/shard_map/ppermute | solution.py:21
  106.7 9.8 %copy-start.2 = (f32[2,8,64,128]{3,2,1,0:T(8,128)S(1)}, f32[2,8,64,128]{3,2,1,0:T(8,128)}, u32[]{:S(2)}) copy-start(f32[2,8,64,128]{3,2,1,0:T(8,128)} %copy-done.1) | copy-start | bytes 1572868
  121.5 11.5 %copy-start.8 = (f32[2,8,64,128]{3,2,1,0:T(8,128)}, f32[2,8,64,128]{3,2,1,0:T(8,128)S(1)}, u32[]{:S(2)}) copy-start(f32[2,8,64,128]{3,2,1,0:T(8,128)S(1)} %multiply_add_fusion.1) | copy-start | bytes 1572868
  121.6 68.3 %collective-permute-start.16 = (f32[2,2,64,128]{3,2,1,0:T(8,128)S(1)}, f32[2,2,64,128]{3,2,1,0:T(8,128)S(1)}, u32[]{:S(2)}, u32[]{:S(2)}) collective-permute-start(f32[2,2,64,128]{3,2,1,0:T(8,128)S(1)} %get-tuple-element.24), channel_id=1, source_target_pairs={{0,1},{1,2},{2,3},{3,4},{4,5},{5,6},{6,7},{7,8},{8,9},{9,10},{10,1... | collective-permute-start | bytes 393224 | tf_op jit(solution)/shard_map/ppermute | solution.py:20
  130.6 59.3 %collective-permute-start.17 = (f32[2,2,64,128]{3,2,1,0:T(8,128)S(1)}, f32[2,2,64,128]{3,2,1,0:T(8,128)S(1)}, u32[]{:S(2)}, u32[]{:S(2)}) collective-permute-start(f32[2,2,64,128]{3,2,1,0:T(8,128)S(1)} %get-tuple-element.25), channel_id=1, source_target_pairs={{1,0},{2,1},{3,2},{4,3},{5,4},{6,5},{7,6},{8,7},{9,8},{10,9},{11,1... | collective-permute-start | bytes 393224 | tf_op jit(solution)/shard_map/ppermute | solution.py:21
  152.1 9.1 copy-start.6
  171.2 9.1 copy-start.9
  194.1 9.2 copy-start.23
  203.2 13.8 %copy-start.36 = (f32[2,8,64,128]{3,2,1,0:T(8,128)S(1)}, f32[2,8,64,128]{3,2,1,0:T(8,128)}, u32[]{:S(2)}) copy-start(f32[2,8,64,128]{3,2,1,0:T(8,128)} %param.16) | copy-start | bytes 1572868
  203.3 6.3 collective-permute-start
  207.1 10.0 %collective-permute-start.1 = (f32[2,2,64,128]{3,2,1,0:T(8,128)S(1)}, f32[2,2,64,128]{3,2,1,0:T(8,128)S(1)}, u32[]{:S(2)}, u32[]{:S(2)}) collective-permute-start(f32[2,2,64,128]{3,2,1,0:T(8,128)S(1)} %get-tuple-element.43), channel_id=1, source_target_pairs={{1,0},{2,1},{3,2},{4,3},{5,4},{6,5},{7,6},{8,7},{9,8},{10,9},{11,1... | collective-permute-start | bytes 393224 | tf_op jit(solution)/shard_map/ppermute | solution.py:21
  225.5 4.4 collective-permute-start.18
  227.4 12.3 %collective-permute-start.19 = (f32[2,2,64,128]{3,2,1,0:T(8,128)S(1)}, f32[2,2,64,128]{3,2,1,0:T(8,128)S(1)}, u32[]{:S(2)}, u32[]{:S(2)}) collective-permute-start(f32[2,2,64,128]{3,2,1,0:T(8,128)S(1)} %get-tuple-element.23), channel_id=1, source_target_pairs={{1,0},{2,1},{3,2},{4,3},{5,4},{6,5},{7,6},{8,7},{9,8},{10,9},{11,1... | collective-permute-start | bytes 393224 | tf_op jit(solution)/shard_map/ppermute | solution.py:21
  247.9 4.4 collective-permute-start.20
  249.9 12.3 %collective-permute-start.21 = (f32[2,2,64,128]{3,2,1,0:T(8,128)S(1)}, f32[2,2,64,128]{3,2,1,0:T(8,128)S(1)}, u32[]{:S(2)}, u32[]{:S(2)}) collective-permute-start(f32[2,2,64,128]{3,2,1,0:T(8,128)S(1)} %get-tuple-element.21), channel_id=1, source_target_pairs={{1,0},{2,1},{3,2},{4,3},{5,4},{6,5},{7,6},{8,7},{9,8},{10,9},{11,1... | collective-permute-start | bytes 393224 | tf_op jit(solution)/shard_map/ppermute | solution.py:21
  270.4 6.0 collective-permute-start.22
  274.5 18.2 %collective-permute-start.23 = (f32[2,2,64,128]{3,2,1,0:T(8,128)S(1)}, f32[2,2,64,128]{3,2,1,0:T(8,128)S(1)}, u32[]{:S(2)}, u32[]{:S(2)}) collective-permute-start(f32[2,2,64,128]{3,2,1,0:T(8,128)S(1)} %get-tuple-element.19), channel_id=1, source_target_pairs={{1,0},{2,1},{3,2},{4,3},{5,4},{6,5},{7,6},{8,7},{9,8},{10,9},{11,1... | collective-permute-start | bytes 393224 | tf_op jit(solution)/shard_map/ppermute | solution.py:21
  301.6 6.5 collective-permute-start.24
  303.5 12.3 %collective-permute-start.25 = (f32[2,2,64,128]{3,2,1,0:T(8,128)}, f32[2,2,64,128]{3,2,1,0:T(8,128)}, u32[]{:S(2)}, u32[]{:S(2)}) collective-permute-start(f32[2,2,64,128]{3,2,1,0:T(8,128)} %get-tuple-element.17), channel_id=1, source_target_pairs={{1,0},{2,1},{3,2},{4,3},{5,4},{6,5},{7,6},{8,7},{9,8},{10,9},{11,1... | collective-permute-start | bytes 393224 | tf_op jit(solution)/shard_map/ppermute | solution.py:21
  325.9 10.4 %collective-permute-start.26 = (f32[2,2,64,128]{3,2,1,0:T(8,128)}, f32[2,2,64,128]{3,2,1,0:T(8,128)S(1)}, u32[]{:S(2)}, u32[]{:S(2)}) collective-permute-start(f32[2,2,64,128]{3,2,1,0:T(8,128)} %get-tuple-element.14), channel_id=1, source_target_pairs={{0,1},{1,2},{2,3},{3,4},{4,5},{5,6},{6,7},{7,8},{8,9},{9,10},{10,1... | collective-permute-start | bytes 393224 | tf_op jit(solution)/shard_map/ppermute | solution.py:20
  327.8 12.6 %collective-permute-start.27 = (f32[2,2,64,128]{3,2,1,0:T(8,128)}, f32[2,2,64,128]{3,2,1,0:T(8,128)}, u32[]{:S(2)}, u32[]{:S(2)}) collective-permute-start(f32[2,2,64,128]{3,2,1,0:T(8,128)} %get-tuple-element.15), channel_id=1, source_target_pairs={{1,0},{2,1},{3,2},{4,3},{5,4},{6,5},{7,6},{8,7},{9,8},{10,9},{11,1... | collective-permute-start | bytes 393224 | tf_op jit(solution)/shard_map/ppermute | solution.py:21
  342.1 15.2 %copy-start.26 = (f32[2,65536]{1,0:T(2,128)S(1)}, f32[2,65536]{1,0:T(2,128)}, u32[]{:S(2)}) copy-start(f32[2,65536]{1,0:T(2,128)} %reshape.223) | copy-start | bytes 1572868
  349.5 7.7 copy-start.19
  349.6 7.7 copy-start.21
  349.6 7.7 copy-start.25
  350.4 11.1 %collective-permute-start.28 = (f32[2,2,64,128]{3,2,1,0:T(8,128)}, f32[2,2,64,128]{3,2,1,0:T(8,128)S(1)}, u32[]{:S(2)}, u32[]{:S(2)}) collective-permute-start(f32[2,2,64,128]{3,2,1,0:T(8,128)} %get-tuple-element.12), channel_id=1, source_target_pairs={{0,1},{1,2},{2,3},{3,4},{4,5},{5,6},{6,7},{7,8},{8,9},{9,10},{10,1... | collective-permute-start | bytes 393224 | tf_op jit(solution)/shard_map/ppermute | solution.py:20
  355.3 9.6 %collective-permute-start.29 = (f32[2,2,64,128]{3,2,1,0:T(8,128)}, f32[2,2,64,128]{3,2,1,0:T(8,128)}, u32[]{:S(2)}, u32[]{:S(2)}) collective-permute-start(f32[2,2,64,128]{3,2,1,0:T(8,128)} %get-tuple-element.13), channel_id=1, source_target_pairs={{1,0},{2,1},{3,2},{4,3},{5,4},{6,5},{7,6},{8,7},{9,8},{10,9},{11,1... | collective-permute-start | bytes 393224 | tf_op jit(solution)/shard_map/ppermute | solution.py:21
  374.8 8.3 collective-permute-start.30
  377.9 11.0 %collective-permute-start.31 = (f32[2,2,64,128]{3,2,1,0:T(8,128)S(1)}, f32[2,2,64,128]{3,2,1,0:T(8,128)S(1)}, u32[]{:S(2)}, u32[]{:S(2)}) collective-permute-start(f32[2,2,64,128]{3,2,1,0:T(8,128)S(1)} %get-tuple-element.11), channel_id=1, source_target_pairs={{1,0},{2,1},{3,2},{4,3},{5,4},{6,5},{7,6},{8,7},{9,8},{10,9},{11,1... | collective-permute-start | bytes 393224 | tf_op jit(solution)/shard_map/ppermute | solution.py:21
  401.3 427.3 %copy-start.37 = (f32[8,64,128]{2,1,0:T(8,128)S(1)}, f32[8,64,128]{2,1,0:T(8,128)}, u32[]{:S(2)}) copy-start(f32[8,64,128]{2,1,0:T(8,128)} %param.13) | copy-start | bytes 786436
  709.4 215.2 %copy-start.34 = (f32[8,64,128]{2,1,0:T(8,128)S(1)}, f32[8,64,128]{2,1,0:T(8,128)}, u32[]{:S(2)}) copy-start(f32[8,64,128]{2,1,0:T(8,128)} %all-reduce.18.cloned.1.call-done) | copy-start | bytes 786436
  (30 other events, 85.0 us)
Sparse Core Ops, SparseCore 0:
  401.4 307.8 all-reduce.17
where the time goes:
time: 943 us; the launch traced here: 934 us
  waiting for transfers between devices  416 us (44%)
  blocking collectives  211 us (22%)
  local copies, waits for them, and re-layouts  99.7 us (11%)
  other arithmetic  97.8 us (10%)
  starting transfers between devices  88.8 us (9%)
  between operations  19.5 us (2%)
    psum x1, waiting for transfers between devices, shards(): gradient = lax.psum(gradient, 'shot')  308 us
    psum x1, blocking collectives, statistics(): grand_total = lax.psum(jnp.sum(scaled * scaled), ('shot', 'depth'))  117 us
    ppermute x16, waiting for transfers between devices, with_halo(): after = lax.ppermute(leading, axis, down)  108 us
    psum x1, blocking collectives, statistics(): energy = lax.psum(jnp.sum(weight * halfway * halfway), ('shot', 'depth'))  94.6 us
    gather x16, local copies, waits for them, and re-layouts, sample(): values = jnp.take_along_axis(field.reshape(shot_count, -1), target, axis=1)  73 us
    unnamed x14, other arithmetic  61 us
    ppermute x16, starting transfers between devices, with_halo(): before = lax.ppermute(last, axis, up)  49 us
    ppermute x16, starting transfers between devices, with_halo(): after = lax.ppermute(leading, axis, down)  39.8 us
  transfers between devices with their start and end apart: 33, of which 15 were waited for; matrix products, arithmetic and copies ran while one was open for 9% of the time, Pallas kernels for 0%

commit v1 on v0

v1 whole, which is shorter than its diff:
```python
import jax
import jax.numpy as jnp
from jax import lax
from jax.experimental import pallas as pl
from jax.experimental.pallas import tpu as pltpu
from jax.sharding import PartitionSpec as P

MESH = pl.DeviceIdType.MESH
CENTER = -2.5
NEAR = 4.0 / 3.0
FAR = -1.0 / 12.0
AMPLITUDE = 100.0
EPSILON = 1e-06

SHOTS = 2
PLANES = 8
ROWS = 64
LANES = 128
STEPS = 8
HALO = 4
PAD = 8
EXT = PLANES + 4
NREC = 512


def window_kernel(
    c_in, fprev, fcur, anext, acur, observed, src, rec, ckpt,
    grad_out,
    u, p, lap, obs, cnt, hot, cs, grad, wave, stage_next, stage_cur,
    local_sem, send_sem, recv_sem, init_send, init_recv,
):
    s = lax.axis_index("shot")
    d = lax.axis_index("depth")
    size = lax.axis_size("depth")
    odd = lax.rem(d, 2)
    early_side, late_side = 1 - odd, odd
    early_id = (s, d + 1 - 2 * odd)
    has_late = ((odd == 1) & (d < size - 1)) | ((odd == 0) & (d > 0))
    late_id = (s, jnp.clip(d - 1 + 2 * odd, 0, size - 1))

    barrier = pltpu.get_barrier_semaphore()
    pl.semaphore_signal(barrier, inc=1, device_id=early_id, device_id_type=MESH)

    @pl.when(has_late)
    def _():
        pl.semaphore_signal(barrier, inc=1, device_id=late_id, device_id_type=MESH)

    data = pl.ds(PAD, ROWS)
    own = pl.ds(HALO, PLANES)
    loads = [
        pltpu.make_async_copy(fcur, u.at[1, :, own, data, :], local_sem.at[0]),
        pltpu.make_async_copy(fprev, u.at[0, :, own, data, :], local_sem.at[1]),
        pltpu.make_async_copy(c_in, cs.at[pl.ds(2, PLANES)], local_sem.at[2]),
        pltpu.make_async_copy(acur, stage_cur, local_sem.at[3]),
        pltpu.make_async_copy(anext, stage_next, local_sem.at[4]),
    ]
    for copy in loads:
        copy.start()

    pl.semaphore_wait(barrier, jnp.where(has_late, 2, 1))

    def first_copies(side, target):
        other = 1 - side
        out = []
        for width, source, slot, level in ((4, fcur, 0, 1), (2, fprev, 1, 0)):
            for shot in range(SHOTS):
                out.append(
                    pltpu.make_async_remote_copy(
                        source.at[shot, pl.ds((PLANES - width) * side, width)],
                        u.at[level, shot, pl.ds(HALO - width + (PLANES + width) * other, width), data, :],
                        init_send.at[slot, shot, side],
                        init_recv.at[slot, shot, other],
                        device_id=target,
                        device_id_type=MESH,
                    )
                )
        out.append(
            pltpu.make_async_remote_copy(
                c_in.at[pl.ds((PLANES - 2) * side, 2)],
                cs.at[pl.ds((PLANES + 2) * other, 2)],
                init_send.at[2, 0, side],
                init_recv.at[2, 0, other],
                device_id=target,
                device_id_type=MESH,
            )
        )
        return out

    def adj_copies(side, target):
        other = 1 - side
        return [
            pltpu.make_async_remote_copy(
                p.at[8, shot, pl.ds(HALO + (PLANES - 2) * side, 2), data, :],
                p.at[8, shot, pl.ds(HALO - 2 + (PLANES + 2) * other, 2), data, :],
                init_send.at[3, shot, side],
                init_recv.at[3, shot, other],
                device_id=target,
                device_id_type=MESH,
            )
            for shot in range(SHOTS)
        ]

    def halo_copy(buf, level, slot, shot, side, width, target):
        other = 1 - side
        return pltpu.make_async_remote_copy(
            buf.at[level, shot, pl.ds(HALO + (PLANES - width) * side, width), data, :],
            buf.at[level, shot, pl.ds(HALO - width + (PLANES + width) * other, width), data, :],
            send_sem.at[slot, shot, side],
            recv_sem.at[slot, shot, other],
            device_id=target,
            device_id_type=MESH,
        )

    @pl.when(has_late)
    def _():
        for copy in first_copies(late_side, late_id):
            copy.start()

    for copy in first_copies(early_side, early_id):
        copy.start()

    loads[2].wait()
    loads[3].wait()
    loads[4].wait()

    def scale(i, carry):
        factor = cs[2 + i]
        for shot in range(SHOTS):
            p[9, shot, HALO + i, PAD : PAD + ROWS, :] = factor * stage_next[shot, i]
            p[8, shot, HALO + i, PAD : PAD + ROWS, :] = factor * stage_cur[shot, i]
        return carry

    lax.fori_loop(0, PLANES, scale, 0)

    @pl.when(has_late)
    def _():
        for copy in adj_copies(late_side, late_id):
            copy.start()

    for copy in adj_copies(early_side, early_id):
        copy.start()

    def clear_pads(i, carry):
        level, plane = i // (PLANES + 2 * HALO), lax.rem(i, PLANES + 2 * HALO)
        zeros = jnp.zeros((PAD, LANES), jnp.float32)
        for buf in (u, p):
            for shot in range(SHOTS):
                buf[level, shot, plane, 0:PAD, :] = zeros
                buf[level, shot, plane, PAD + ROWS : 2 * PAD + ROWS, :] = zeros
        return carry

    lax.fori_loop(0, 10 * (PLANES + 2 * HALO), clear_pads, 0)

    @pl.when(jnp.logical_not(has_late))
    def _():
        first = (PLANES + HALO) * late_side

        def clear(i, carry):
            level, plane = i // HALO, first + lax.rem(i, HALO)
            zeros = jnp.zeros((ROWS, LANES), jnp.float32)
            for buf in (u, p):
                for shot in range(SHOTS):
                    buf[level, shot, plane, PAD : PAD + ROWS, :] = zeros
            return carry

        lax.fori_loop(0, 10 * HALO, clear, 0)
        for i in range(2):
            cs[(PLANES + 2) * late_side + i] = jnp.zeros((ROWS, LANES), jnp.float32)

    grad[...] = jnp.zeros_like(grad)

    for k in range(STEPS):
        cycle = lax.rem(ckpt[0] + k, 48).astype(jnp.float32)
        a = (jnp.full((1, LANES), cycle, jnp.float32) - 24.0) / 12.0
        wave[k : k + 1, :] = AMPLITUDE * (1.0 - 2.0 * a * a) * jnp.exp(-a * a)

    first_cell = (d * PLANES - 2) * (ROWS * LANES)
    rows_ext = EXT * ROWS
    row_at = lax.broadcasted_iota(jnp.int32, (rows_ext, NREC), 0)
    lane_at = lax.broadcasted_iota(jnp.int32, (LANES, NREC), 0)
    nt = (((1,), (1,)), ((), ()))

    def place(shot, carry):
        cell = rec[pl.ds(shot, 1), :] - first_cell
        row = lax.shift_right_arithmetic(cell, 7)
        lane = lax.bitwise_and(cell, 127)
        at_row = jnp.where(row_at == row, 1.0, 0.0).astype(jnp.bfloat16)
        lane_hit = lane_at == lane

        def put(values):
            right = jnp.where(lane_hit, values, 0.0).astype(jnp.bfloat16)
            return lax.dot_general(at_row, right, nt, preferred_element_type=jnp.float32)

        cnt[shot] = put(jnp.ones((1, NREC), jnp.float32)).reshape(EXT, ROWS, LANES)
        for k in range(STEPS):
            trace = observed[shot, k : k + 1, :]
            high = trace.astype(jnp.bfloat16).astype(jnp.float32)
            total = put(high) + put(trace - high)
            obs[k, shot] = total.reshape(EXT, ROWS, LANES)
        source = src[shot] - first_cell
        inside = lax.broadcasted_iota(jnp.int32, (ROWS, LANES), 0) * LANES + lax.broadcasted_iota(jnp.int32, (ROWS, LANES), 1)
        for plane in range(EXT):
            hot[shot, plane] = jnp.where(inside == source - plane * (ROWS * LANES), 1.0, 0.0)
        return carry

    lax.fori_loop(0, SHOTS, place, 0)

    lane_iota = lax.broadcasted_iota(jnp.int32, (ROWS, LANES), 1)
    masks = {j: (lane_iota >= j) if j > 0 else (lane_iota < LANES + j) for j in (1, 2, -1, -2)}

    def laplace(buf, level, shot, plane):
        def at(dz, dx):
            return buf[level, shot, plane + dz, PAD + dx : PAD + dx + ROWS, :]

        center = at(0, 0)

        def along_y(j):
            return jnp.where(masks[j], pltpu.roll(center, j % LANES, 1), 0.0)

        near = (at(-1, 0) + at(1, 0)) + (at(0, -1) + at(0, 1)) + (along_y(1) + along_y(-1))
        far = (at(-2, 0) + at(2, 0)) + (at(0, -2) + at(0, 2)) + (along_y(2) + along_y(-2))
        return center, 3.0 * CENTER * center + NEAR * near + FAR * far

    def forward(k, shot, start, count):
        strength = wave[pl.ds(k, 1), :]

        def one(i, carry):
            plane = start + i
            center, value = laplace(u, k + 1, shot, plane)
            value = value + strength * hot[shot, plane - 2]
            lap[k, shot, plane - 2] = value
            older = u[k, shot, plane, PAD : PAD + ROWS, :]
            u[k + 2, shot, plane, PAD : PAD + ROWS, :] = 2.0 * center - older + cs[plane - 2] * value
            return carry

        lax.fori_loop(0, count, one, 0)

    def backward(k, shot, start, count):
        def one(i, carry):
            plane = start + i
            center, value = laplace(p, k + 1, shot, plane)
            ahead = u[k + 2, shot, plane, PAD : PAD + ROWS, :]
            value = value + (cnt[shot, plane - 2] * ahead - obs[k, shot, plane - 2])
            later = p[k + 2, shot, plane, PAD : PAD + ROWS, :]
            newer = 2.0 * center - later + cs[plane - 2] * value
            p[k, shot, plane, PAD : PAD + ROWS, :] = newer
            grad[plane - 2] += newer * lap[k, shot, plane - 2]
            return carry

        lax.fori_loop(0, count, one, 0)

    def when_late(action):
        pl.when(has_late)(action)

    even = 1 - odd
    loads[0].wait()
    loads[1].wait()

    def arrived(buf, level, slot, shot, side, width, target):
        halo_copy(buf, level, slot, shot, 1 - side, width, target).wait_recv()

    def first_arrived(shot, side, target):
        copies = first_copies(1 - side, target)
        copies[shot].wait_recv()
        copies[SHOTS + shot].wait_recv()
        if shot == 0:
            copies[2 * SHOTS].wait_recv()

    def forward_round(j, carry):
        k = 2 * j

        def arrive(shot, side, target):
            @pl.when(j == 0)
            def _():
                first_arrived(shot, side, target)

            @pl.when(j > 0)
            def _():
                arrived(u, k + 1, j, shot, side, 4, target)

        def leave(shot, side, target):
            @pl.when(j < 3)
            def _():
                halo_copy(u, k + 3, j + 1, shot, side, 4, target).start()

        for shot in range(SHOTS):
            arrive(shot, early_side, early_id)
            forward(k, shot, 2 + 4 * even, 8)
            forward(k + 1, shot, 4 + 4 * even, 4)
            leave(shot, early_side, early_id)
        for shot in range(SHOTS):
            when_late(lambda: arrive(shot, late_side, late_id))
            forward(k, shot, 2 + 8 * odd, 4)
            forward(k + 1, shot, 4 + 4 * odd, 4)
            when_late(lambda: leave(shot, late_side, late_id))
        return carry

    lax.fori_loop(0, 4, forward_round, 0)

    def adj_arrived(shot, side, target):
        adj_copies(1 - side, target)[shot].wait_recv()

    for shot in range(SHOTS):
        adj_arrived(shot, early_side, early_id)
        backward(7, shot, 4 + 2 * even, 6)
        halo_copy(p, 7, 4, shot, early_side, 4, early_id).start()
    for shot in range(SHOTS):
        when_late(lambda: adj_arrived(shot, late_side, late_id))
        backward(7, shot, 4 + 6 * odd, 2)
        when_late(lambda: halo_copy(p, 7, 4, shot, late_side, 4, late_id).start())

    def backward_round(i, carry):
        k = 6 - 2 * i

        def leave(shot, side, target):
            @pl.when(i < 2)
            def _():
                halo_copy(p, k - 1, 5 + i, shot, side, 4, target).start()

            @pl.when(i == 2)
            def _():
                halo_copy(p, k - 1, 5 + i, shot, side, 2, target).start()

        for shot in range(SHOTS):
            arrived(p, k + 1, 4 + i, shot, early_side, 4, early_id)
            backward(k, shot, 2 + 4 * even, 8)
            backward(k - 1, shot, 4 + 4 * even, 4)
            leave(shot, early_side, early_id)
        for shot in range(SHOTS):
            when_late(lambda: arrived(p, k + 1, 4 + i, shot, late_side, 4, late_id))
            backward(k, shot, 2 + 8 * odd, 4)
            backward(k - 1, shot, 4 + 4 * odd, 4)
            when_late(lambda: leave(shot, late_side, late_id))
        return carry

    lax.fori_loop(0, 3, backward_round, 0)

    for shot in range(SHOTS):
        arrived(p, 1, 7, shot, early_side, 2, early_id)
        backward(0, shot, 4 + 2 * even, 6)
    for shot in range(SHOTS):
        when_late(lambda: arrived(p, 1, 7, shot, late_side, 2, late_id))
        backward(0, shot, 4 + 6 * odd, 2)

    def finish(i, carry):
        grad_out[i] = grad[2 + i] / cs[2 + i]
        return carry

    lax.fori_loop(0, PLANES, finish, 0)

    def sent(side, target):
        for copy in first_copies(side, target) + adj_copies(side, target):
            copy.wait_send()
        for shot in range(SHOTS):
            for slot, buf, level in ((1, u, 3), (2, u, 5), (3, u, 7), (4, p, 7), (5, p, 5), (6, p, 3)):
                halo_copy(buf, level, slot, shot, side, 4, target).wait_send()
            halo_copy(p, 1, 7, shot, side, 2, target).wait_send()

    sent(early_side, early_id)
    when_late(lambda: sent(late_side, late_id))


def window(c, fprev, fcur, anext, acur, observed, src, rec, ckpt):
    any_space = pl.BlockSpec(memory_space=pl.ANY)
    in_vmem = pl.BlockSpec(memory_space=pltpu.VMEM)
    in_smem = pl.BlockSpec(memory_space=pltpu.SMEM)
    padded = (10, SHOTS, PLANES + 2 * HALO, ROWS + 2 * PAD, LANES)
    f32 = jnp.float32
    return pl.pallas_call(
        window_kernel,
        out_shape=jax.ShapeDtypeStruct((PLANES, ROWS, LANES), f32),
        in_specs=[any_space] * 5 + [in_vmem, in_smem, in_vmem, in_smem],
        out_specs=in_vmem,
        scratch_shapes=[
            pltpu.VMEM(padded, f32),
            pltpu.VMEM(padded, f32),
            pltpu.VMEM((STEPS, SHOTS, EXT, ROWS, LANES), f32),
            pltpu.VMEM((STEPS, SHOTS, EXT, ROWS, LANES), f32),
            pltpu.VMEM((SHOTS, EXT, ROWS, LANES), f32),
            pltpu.VMEM((SHOTS, EXT, ROWS, LANES), f32),
            pltpu.VMEM((EXT, ROWS, LANES), f32),
            pltpu.VMEM((EXT, ROWS, LANES), f32),
            pltpu.VMEM((STEPS, LANES), f32),
            pltpu.VMEM((SHOTS, PLANES, ROWS, LANES), f32),
            pltpu.VMEM((SHOTS, PLANES, ROWS, LANES), f32),
            pltpu.SemaphoreType.DMA((5,)),
            pltpu.SemaphoreType.DMA((8, SHOTS, 2)),
            pltpu.SemaphoreType.DMA((8, SHOTS, 2)),
            pltpu.SemaphoreType.DMA((4, SHOTS, 2)),
            pltpu.SemaphoreType.DMA((4, SHOTS, 2)),
        ],
        compiler_params=pltpu.CompilerParams(
            collective_id=0, has_side_effects=True, vmem_limit_bytes=60 * 1024 * 1024
        ),
        name="window",
    )(c, fprev, fcur, anext, acur, observed, src, rec, ckpt)


def reduce_kernel(
    grad, moment, half_out, kinetic_out,
    parts, scaled, tiles, depth_tiles,
    send_sem, recv_sem,
):
    s, d = lax.axis_index("shot"), lax.axis_index("depth")
    ns, nd = lax.axis_size("shot"), lax.axis_size("depth")
    per_plane = ns // PLANES
    cells_all = nd * PLANES * ROWS * LANES

    def shot_peers(action):
        def one(r, carry):
            action(lax.rem(s + r, ns))
            return carry

        lax.fori_loop(1, ns, one, 0)

    def depth_peers(action):
        def one(r, carry):
            action(lax.rem(d + r, nd))
            return carry

        lax.fori_loop(1, nd, one, 0)

    barrier = pltpu.get_barrier_semaphore()
    shot_peers(lambda j: pl.semaphore_signal(barrier, inc=1, device_id=(j, d), device_id_type=MESH))
    depth_peers(lambda j: pl.semaphore_signal(barrier, inc=1, device_id=(s, j), device_id_type=MESH))
    pl.semaphore_wait(barrier, ns + nd - 2)

    def remote(source, target, sem, device):
        return pltpu.make_async_remote_copy(
            source, target, send_sem.at[sem], recv_sem.at[sem], device_id=device, device_id_type=MESH
        )

    shot_peers(lambda j: remote(grad.at[j], parts.at[s], 0, (j, d)).start())
    parts[s] = grad[s]
    every = pl.ds(0, ns - 1)
    remote(parts.at[every], parts.at[every], 0, (s, d)).wait_recv()
    total = lax.fori_loop(1, ns, lambda j, t: t + parts[j], parts[0])
    plane = d * PLANES + s // per_plane
    weight = 1.0 + 2.0 * plane.astype(jnp.float32) / (nd * PLANES - 1)
    mine = weight * total
    scaled[s] = mine
    old = moment[s]
    sums = (jnp.sum(mine * mine), weight * jnp.sum(old * old), weight * jnp.sum(old * mine), weight * jnp.sum(mine * mine))
    for q, value in enumerate(sums):
        tiles[s, q : q + 1, :] = jnp.full((1, LANES), value, jnp.float32)
    tiles[s, 4:8, :] = jnp.zeros((4, LANES), jnp.float32)
    shot_peers(lambda j: remote(tiles.at[s], tiles.at[s], 1, (j, d)).start())
    shot_peers(lambda j: remote(scaled.at[s], scaled.at[s], 2, (j, d)).start())
    remote(tiles.at[every], tiles.at[every], 1, (s, d)).wait_recv()
    depth_tiles[d] = lax.fori_loop(1, ns, lambda j, t: t + tiles[j], tiles[0])
    depth_peers(lambda j: remote(depth_tiles.at[d], depth_tiles.at[d], 3, (s, j)).start())
    others = pl.ds(0, nd - 1)
    remote(depth_tiles.at[others], depth_tiles.at[others], 3, (s, d)).wait_recv()
    grand = lax.fori_loop(1, nd, lambda j, t: t + depth_tiles[j], depth_tiles[0])
    step = 0.5 * lax.rsqrt(grand[0:1, :] / cells_all + EPSILON)
    energy = grand[1:2, :] - 2.0 * step * grand[2:3, :] + step * step * grand[3:4, :]
    kinetic_out[...] = 0.5 * energy / cells_all
    remote(scaled.at[every], scaled.at[every], 2, (s, d)).wait_recv()

    def update(j, carry):
        half_out[j] = moment[j] - step * scaled[j]
        return carry

    lax.fori_loop(0, ns, update, 0)
    remote(parts.at[every], parts.at[every], 0, (s, d)).wait_send()
    remote(tiles.at[every], tiles.at[every], 1, (s, d)).wait_send()
    remote(scaled.at[every], scaled.at[every], 2, (s, d)).wait_send()
    remote(depth_tiles.at[others], depth_tiles.at[others], 3, (s, d)).wait_send()


def reduce_and_step(grad, momentum, ns, nd):
    in_vmem = pl.BlockSpec(memory_space=pltpu.VMEM)
    f32 = jnp.float32
    blocks = (ns, PLANES * ROWS // ns, LANES)
    half, kinetic = pl.pallas_call(
        reduce_kernel,
        out_shape=(jax.ShapeDtypeStruct(blocks, f32), jax.ShapeDtypeStruct((1, LANES), f32)),
        in_specs=[in_vmem] * 2,
        out_specs=(in_vmem, in_vmem),
        scratch_shapes=[
            pltpu.VMEM(blocks, f32),
            pltpu.VMEM(blocks, f32),
            pltpu.VMEM((ns, 8, LANES), f32),
            pltpu.VMEM((nd, 8, LANES), f32),
            pltpu.SemaphoreType.DMA((4,)),
            pltpu.SemaphoreType.DMA((4,)),
        ],
        compiler_params=pltpu.CompilerParams(collective_id=1, has_side_effects=True),
        name="reduce",
    )(grad.reshape(blocks), momentum.reshape(blocks))
    return half.reshape(momentum.shape), kinetic[0, 0]


def solution(mesh):
    def shards(c, momentum, fprev, fcur, anext, acur, observed, src, rec, ckpt):
        grad = window(c, fprev, fcur, anext, acur, observed, src, rec, ckpt.reshape(1))
        return reduce_and_step(grad, momentum, mesh.shape["shot"], mesh.shape["depth"])

    placed = (
        P("depth", None, None),
        P("depth", None, None),
        P("shot", "depth", None, None),
        P("shot", "depth", None, None),
        P("shot", "depth", None, None),
        P("shot", "depth", None, None),
        P("shot", None, None),
        P("shot"),
        P("shot", None),
        P(),
    )
    return jax.shard_map(
        shards, mesh=mesh, in_specs=placed, out_specs=(P("depth", None, None), P()), check_vma=False
    )
```

time: 943 us -> 126 us (0.13)
  waiting for transfers between devices: 416 us -> 0 us
  blocking collectives: 211 us -> 0 us
  Pallas kernels: 0 us -> 122 us
  local copies, waits for them, and re-layouts: 99.7 us -> 1.68 us
  other arithmetic: 97.8 us -> 0 us
  starting transfers between devices: 88.8 us -> 0 us
  between operations: 19.5 us -> 2.47 us
    psum x1 -> x0, waiting for transfers between devices: 308 us -> none  [shards(): gradient = lax.psum(gradient, 'shot')]
    psum x2 -> x0, blocking collectives: 211 us -> none  [the longest x1 117 us: statistics(): grand_total = lax.psum(jnp.sum(scaled * scaled), ('shot', 'depth'))]
    pallas_call x0 -> x2, Pallas kernels: none -> 122 us  [the longest x1 63.1 us: reduce_and_step(): pl.pallas_call(reduce_kernel, out_shape=(jax.ShapeDtypeStruct(blocks, f32...]
    ppermute x32 -> x0, waiting for transfers between devices: 108 us -> none  [the longest x16 108 us: with_halo(): after = lax.ppermute(leading, axis, down)]
    ppermute x32 -> x0, starting transfers between devices: 88.7 us -> none  [the longest x16 49 us: with_halo(): before = lax.ppermute(last, axis, up)]
    gather x16 -> x0, local copies, waits for them, and re-layouts: 73 us -> none  [sample(): values = jnp.take_along_axis(field.reshape(shot_count, -1), target, axis=1)]
    unnamed x14 -> x0, other arithmetic: 61 us -> none
    add x26 -> x0, other arithmetic: 15.9 us -> none  [the longest x8 7.99 us: shards(): adj_new = 2.0 * adj_now - adj_later + laplace(padded)]
  transfers between devices with their start and end apart: 33 -> 0, of which waited for: 15 -> 0; matrix products, arithmetic and copies ran while one was open for 9% -> 0% of each run, Pallas kernels for 0% -> 0%
where the time goes in v1:
time: 126 us
  Pallas kernels  122 us (97%)
  between operations  2.47 us (2%)
  local copies, waits for them, and re-layouts  1.68 us (1%)
    pallas_call x1, Pallas kernels, reduce_and_step(): pl.pallas_call(reduce_kernel, out_shape=(jax.ShapeDtypeStruct(blocks, f32...  63.1 us
    pallas_call x1, Pallas kernels, window(): pl.pallas_call(window_kernel, out_shape=jax.ShapeDtypeStruct((PLANES, ROW...  58.4 us

profile of v1, /device:TPU:1, one launch (start us, length us, event | category | flops | bytes accessed | tf_op | source)
XLA Modules:
  0.0 125.7 jit_solution(1570435647754142020)
XLA Ops:
  1.3 58.4 %window.1 = f32[8,64,128]{2,1,0:T(8,128)} custom-call(f32[8,64,128]{2,1,0:T(8,128)} %c_in.1, f32[2,8,64,128]{3,2,1,0:T(8,128)} %fprev.1, f32[2,8,64,128]{3,2,1,0:T(8,128)} %fcur.1, f32[2,8,64,128]{3,2,1,0:T(8,128)} %anext.1, f32[2,8,64,128]{3,2,1,0:T(8,128)} %acur.1, f32[2,8,512]{2,1,0:T(8,128)} %observed.1, s32[2]{0:T(128)} %src.1, s32[2,512]{1,0:T(2,128)} %rec.1, ...), custom_call_target="tpu_custom_call" | custom-call | tf_op jit(solution)/shard_map/window/pallas_call | solution.py:369
  59.7 63.1 %reduce.1 = (f32[32,16,128]{2,1,0:T(8,128)}, f32[1,128]{1,0:T(1,128)}) custom-call(f32[32,16,128]{2,1,0:T(8,128)} %bitcast.7, f32[32,16,128]{2,1,0:T(8,128)} %bitcast.8), custom_call_target="tpu_custom_call" | custom-call | tf_op jit(solution)/shard_map/reduce/pallas_call | solution.py:475
  122.8 0.0 copy-start
  122.8 1.7 %copy.15 = f32[8,64,128]{2,1,0:T(8,128)} copy(f32[8,64,128]{2,1,0:T(8,128)} %bitcast.9) | data formatting | bytes 524288
  124.5 0.0 copy-done
Async XLA Ops:
  122.8 1.7 %copy-start = (f32[1,128]{1,0:T(1,128)S(1)}, f32[1,128]{1,0:T(1,128)}, u32[]{:S(2)}) copy-start(f32[1,128]{1,0:T(1,128)} %get-tuple-element.5) | copy-start | bytes 1540

commit v2 on v1

v2 whole, which is shorter than its diff:
```python
import jax
import jax.numpy as jnp
from jax import lax
from jax.experimental import pallas as pl
from jax.experimental.pallas import tpu as pltpu
from jax.sharding import PartitionSpec as P

MESH = pl.DeviceIdType.MESH
CENTER = -2.5
NEAR = 4.0 / 3.0
FAR = -1.0 / 12.0
AMPLITUDE = 100.0
EPSILON = 1e-06

SHOTS = 2
PLANES = 8
ROWS = 64
LANES = 128
STEPS = 8
HALO = 4
PAD = 8
EXT = PLANES + 4
NREC = 512
Z_LO = 4


def window_kernel(
    c_in, fprev, fcur, anext, acur, observed, src, rec, ckpt, moment,
    half_out, kinetic_out,
    u, p, lap, obs, cnt, hot, cs, grad, wave, stage_next, stage_cur,
    blocks, parts, scaled, tiles, depth_tiles,
    relay,
    local_sem, send_sem, recv_sem, init_send, init_recv, parcel_send, parcel_recv, relay_send, relay_recv,
    all_send, all_recv, token,
):
    s = lax.axis_index("shot")
    d = lax.axis_index("depth")
    shots, size = lax.axis_size("shot"), lax.axis_size("depth")
    rows_y, half = shots // Z_LO, size // 2
    y, z_lo, x_core = s // Z_LO, lax.rem(s, Z_LO), lax.rem(d, half)
    odd = lax.rem(d, 2)
    early_side, late_side = 1 - odd, odd
    early_id = (s, d + 1 - 2 * odd)
    has_late = ((odd == 1) & (d < size - 1)) | ((odd == 0) & (d > 0))
    late_id = (s, jnp.clip(d - 1 + 2 * odd, 0, size - 1))

    def each(count, action):
        def one(r, carry):
            action(r)
            return carry

        lax.fori_loop(1, count, one, 0)

    def y_peer(r):
        return (lax.rem(y + r, rows_y) * Z_LO + z_lo, d)

    far_side = (s, lax.rem(d + half, size))
    at_cut = (d == half - 1) | (d == half)

    barrier = pltpu.get_barrier_semaphore()

    def greet(device):
        pl.semaphore_signal(barrier, inc=1, device_id=device, device_id_type=MESH)

    @pl.when(at_cut)
    def _():
        greet((s, size - 1 - d))

    greet(far_side)
    each(rows_y, lambda r: greet(y_peer(r)))
    each(Z_LO, lambda r: greet((y * Z_LO + lax.rem(z_lo + r, Z_LO), d)))
    each(half, lambda r: greet((s, d - x_core + lax.rem(x_core + r, half))))

    data = pl.ds(PAD, ROWS)
    own = pl.ds(HALO, PLANES)
    loads = [
        pltpu.make_async_copy(fcur, u.at[1, :, own, data, :], local_sem.at[0]),
        pltpu.make_async_copy(fprev, u.at[0, :, own, data, :], local_sem.at[1]),
        pltpu.make_async_copy(c_in, cs.at[pl.ds(2, PLANES)], local_sem.at[2]),
        pltpu.make_async_copy(acur, stage_cur, local_sem.at[3]),
        pltpu.make_async_copy(anext, stage_next, local_sem.at[4]),
    ]
    for copy in loads:
        copy.start()

    pl.semaphore_wait(barrier, rows_y + Z_LO + half - 2 + jnp.where(at_cut, 1, 0))

    def copy_to(source, landing, send, recv, target):
        return pltpu.make_async_remote_copy(
            source, landing, send, recv, device_id=target, device_id_type=MESH
        )

    def first_copy(shot, side, target):
        return copy_to(
            fcur.at[shot, pl.ds((PLANES - 2) * side, 2)],
            u.at[1, shot, pl.ds(HALO - 2 + (PLANES + 2) * (1 - side), 2), data, :],
            init_send.at[shot, side], init_recv.at[shot, 1 - side], target,
        )

    def parcel(i, side):
        other = 1 - side
        if i == 0:
            return c_in.at[pl.ds((PLANES - 2) * side, 2)], cs.at[pl.ds((PLANES + 2) * other, 2)], relay.at[pl.ds(0, 2)]
        level, shot = (9, i - 1) if i < 3 else (8, i - 3)
        width = 2 if i < 3 else 4
        return (
            p.at[level, shot, pl.ds(HALO + (PLANES - width) * side, width), data, :],
            p.at[level, shot, pl.ds(HALO - width + (PLANES + width) * other, width), data, :],
            relay.at[pl.ds(2 * i if i < 3 else 4 * i - 6, width)],
        )

    def parcel_copy(i, side, target):
        source, landing, _ = parcel(i, side)
        return copy_to(source, landing, parcel_send.at[i, side], parcel_recv.at[i, 1 - side], target)

    relay_id = (s, jnp.where(d < half, 0, size - 1))
    relays = (d == 0) | (d == size - 1)

    def parcel_to_relay(i, side):
        source, _, middle = parcel(i, side)
        return copy_to(source, middle, parcel_send.at[i, side], relay_recv.at[i], relay_id)

    def parcel_from_relay(i, side):
        _, landing, middle = parcel(i, side)
        return copy_to(middle, landing, relay_send.at[i], parcel_recv.at[i, 1 - side], far_side)

    def post(items):
        for i in items:
            @pl.when(at_cut)
            def _():
                parcel_to_relay(i, late_side).start()

            @pl.when(has_late & jnp.logical_not(at_cut))
            def _():
                parcel_copy(i, late_side, late_id).start()

        for i in items:
            parcel_copy(i, early_side, early_id).start()

    def when_late(action):
        pl.when(has_late)(action)

    def halo_copy(buf, level, slot, shot, side, width, target):
        other = 1 - side
        return pltpu.make_async_remote_copy(
            buf.at[level, shot, pl.ds(HALO + (PLANES - width) * side, width), data, :],
            buf.at[level, shot, pl.ds(HALO - width + (PLANES + width) * other, width), data, :],
            send_sem.at[slot, shot, side],
            recv_sem.at[slot, shot, other],
            device_id=target,
            device_id_type=MESH,
        )

    for shot in range(SHOTS):
        when_late(lambda: first_copy(shot, late_side, late_id).start())
    for shot in range(SHOTS):
        first_copy(shot, early_side, early_id).start()
    post((0,))

    def pass_on(device):
        pl.semaphore_signal(token, inc=1, device_id=device, device_id_type=MESH)

    each(rows_y, lambda r: pass_on(y_peer(r)))
    pass_on(far_side)

    loads[2].wait()
    loads[3].wait()
    loads[4].wait()

    def scale(i, carry):
        factor = cs[2 + i]
        for shot in range(SHOTS):
            p[9, shot, HALO + i, PAD : PAD + ROWS, :] = factor * stage_next[shot, i]
            p[8, shot, HALO + i, PAD : PAD + ROWS, :] = factor * stage_cur[shot, i]
        return carry

    lax.fori_loop(0, PLANES, scale, 0)

    post(range(1, 5))

    def clear_pads(i, carry):
        level, plane = i // (PLANES + 2 * HALO), lax.rem(i, PLANES + 2 * HALO)
        zeros = jnp.zeros((PAD, LANES), jnp.float32)
        for buf in (u, p):
            for shot in range(SHOTS):
                buf[level, shot, plane, 0:PAD, :] = zeros
                buf[level, shot, plane, PAD + ROWS : 2 * PAD + ROWS, :] = zeros
        return carry

    lax.fori_loop(0, 10 * (PLANES + 2 * HALO), clear_pads, 0)

    @pl.when(jnp.logical_not(has_late))
    def _():
        first = (PLANES + HALO) * late_side

        def clear(i, carry):
            level, plane = i // HALO, first + lax.rem(i, HALO)
            zeros = jnp.zeros((ROWS, LANES), jnp.float32)
            for buf in (u, p):
                for shot in range(SHOTS):
                    buf[level, shot, plane, PAD : PAD + ROWS, :] = zeros
            return carry

        lax.fori_loop(0, 10 * HALO, clear, 0)
        for i in range(2):
            cs[(PLANES + 2) * late_side + i] = jnp.zeros((ROWS, LANES), jnp.float32)

    grad[...] = jnp.zeros_like(grad)

    for k in range(STEPS):
        cycle = lax.rem(ckpt[0] + k, 48).astype(jnp.float32)
        a = (jnp.full((1, LANES), cycle, jnp.float32) - 24.0) / 12.0
        wave[k : k + 1, :] = AMPLITUDE * (1.0 - 2.0 * a * a) * jnp.exp(-a * a)

    first_cell = (d * PLANES - 2) * (ROWS * LANES)
    rows_ext = EXT * ROWS
    row_at = lax.broadcasted_iota(jnp.int32, (rows_ext, NREC), 0)
    lane_at = lax.broadcasted_iota(jnp.int32, (LANES, NREC), 0)
    nt = (((1,), (1,)), ((), ()))

    def place(shot, carry):
        cell = rec[pl.ds(shot, 1), :] - first_cell
        row = lax.shift_right_arithmetic(cell, 7)
        lane = lax.bitwise_and(cell, 127)
        at_row = jnp.where(row_at == row, 1.0, 0.0).astype(jnp.bfloat16)
        lane_hit = lane_at == lane

        def put(values):
            right = jnp.where(lane_hit, values, 0.0).astype(jnp.bfloat16)
            return lax.dot_general(at_row, right, nt, preferred_element_type=jnp.float32)

        cnt[shot] = put(jnp.ones((1, NREC), jnp.float32)).reshape(EXT, ROWS, LANES)
        for k in range(STEPS):
            trace = observed[shot, k : k + 1, :]
            high = trace.astype(jnp.bfloat16).astype(jnp.float32)
            total = put(high) + put(trace - high)
            obs[k, shot] = total.reshape(EXT, ROWS, LANES)
        source = src[shot] - first_cell
        inside = lax.broadcasted_iota(jnp.int32, (ROWS, LANES), 0) * LANES + lax.broadcasted_iota(jnp.int32, (ROWS, LANES), 1)
        for plane in range(EXT):
            hot[shot, plane] = jnp.where(inside == source - plane * (ROWS * LANES), 1.0, 0.0)
        return carry

    lax.fori_loop(0, SHOTS, place, 0)

    lane_iota = lax.broadcasted_iota(jnp.int32, (ROWS, LANES), 1)
    masks = {j: (lane_iota >= j) if j > 0 else (lane_iota < LANES + j) for j in (1, 2, -1, -2)}

    def laplaces(buf, level, shot, start, count):
        def at(plane, dx):
            return buf[level, shot, start + plane, PAD + dx : PAD + dx + ROWS, :]

        def along_y(value, j):
            return jnp.where(masks[j], pltpu.roll(value, j % LANES, 1), 0.0)

        planes = {i: at(i, 0) for i in range(-2, count + 2)}
        out = []
        for i in range(count):
            center = planes[i]
            near = (planes[i - 1] + planes[i + 1]) + (at(i, -1) + at(i, 1)) + (along_y(center, 1) + along_y(center, -1))
            far = (planes[i - 2] + planes[i + 2]) + (at(i, -2) + at(i, 2)) + (along_y(center, 2) + along_y(center, -2))
            out.append((center, 3.0 * CENTER * center + NEAR * near + FAR * far))
        return out

    def forward(k, shot, start, count):
        strength = wave[pl.ds(k, 1), :]
        done = []
        for i, (center, value) in enumerate(laplaces(u, k + 1, shot, start, count)):
            plane = start + i
            value = value + strength * hot[shot, plane - 2]
            older = u[k, shot, plane, PAD : PAD + ROWS, :]
            done.append((plane, value, 2.0 * center - older + cs[plane - 2] * value))
        for plane, value, newer in done:
            lap[k, shot, plane - 2] = value
            u[k + 2, shot, plane, PAD : PAD + ROWS, :] = newer

    def backward(k, shot, start, count):
        done = []
        for i, (center, value) in enumerate(laplaces(p, k + 1, shot, start, count)):
            plane = start + i
            ahead = u[k + 2, shot, plane, PAD : PAD + ROWS, :]
            value = value + (cnt[shot, plane - 2] * ahead - obs[k, shot, plane - 2])
            later = p[k + 2, shot, plane, PAD : PAD + ROWS, :]
            newer = 2.0 * center - later + cs[plane - 2] * value
            done.append((plane, newer, grad[plane - 2] + newer * lap[k, shot, plane - 2]))
        for plane, newer, term in done:
            p[k, shot, plane, PAD : PAD + ROWS, :] = newer
            grad[plane - 2] = term

    even = 1 - odd
    loads[0].wait()
    loads[1].wait()

    def arrived(buf, level, slot, shot, side, width, target):
        halo_copy(buf, level, slot, shot, 1 - side, width, target).wait_recv()

    for shot in range(SHOTS):
        first_copy(shot, 1 - early_side, early_id).wait_recv()
        forward(0, shot, 4 + 2 * even, 6)
        halo_copy(u, 2, 0, shot, early_side, 4, early_id).start()
    for shot in range(SHOTS):
        when_late(lambda: first_copy(shot, 1 - late_side, late_id).wait_recv())
        forward(0, shot, 4 + 6 * odd, 2)
        when_late(lambda: halo_copy(u, 2, 0, shot, late_side, 4, late_id).start())

    @pl.when(relays)
    def _():
        for i in range(5):
            parcel_to_relay(i, early_side).wait_recv()
            parcel_from_relay(i, early_side).start()

    parcel_copy(0, 1 - early_side, early_id).wait_recv()
    when_late(lambda: parcel_copy(0, 1 - late_side, late_id).wait_recv())

    def forward_round(j, carry):
        k = 2 * j + 1

        def leave(shot, side, target):
            @pl.when(j < 3)
            def _():
                halo_copy(u, k + 3, j + 1, shot, side, 4, target).start()

        def second(shot, start):
            @pl.when(j < 3)
            def _():
                forward(k + 1, shot, start, 4)

        for shot in range(SHOTS):
            arrived(u, k + 1, j, shot, early_side, 4, early_id)
            forward(k, shot, 2 + 4 * even, 8)
            second(shot, 4 + 4 * even)
            leave(shot, early_side, early_id)
        for shot in range(SHOTS):
            when_late(lambda: arrived(u, k + 1, j, shot, late_side, 4, late_id))
            forward(k, shot, 2 + 8 * odd, 4)
            second(shot, 4 + 4 * odd)
            when_late(lambda: leave(shot, late_side, late_id))
        return carry

    lax.fori_loop(0, 4, forward_round, 0)

    for i in range(1, 5):
        parcel_copy(i, 1 - early_side, early_id).wait_recv()
        when_late(lambda: parcel_copy(i, 1 - late_side, late_id).wait_recv())

    def backward_round(i, carry):
        k = 7 - 2 * i

        def arrive(shot, side, target):
            @pl.when(i > 0)
            def _():
                arrived(p, k + 1, 3 + i, shot, side, 4, target)

        def leave(shot, side, target):
            @pl.when(i < 3)
            def _():
                halo_copy(p, k - 1, 4 + i, shot, side, 4, target).start()

        for shot in range(SHOTS):
            arrive(shot, early_side, early_id)
            backward(k, shot, 2 + 4 * even, 8)
            backward(k - 1, shot, 4 + 4 * even, 4)
            leave(shot, early_side, early_id)
        for shot in range(SHOTS):
            when_late(lambda: arrive(shot, late_side, late_id))
            backward(k, shot, 2 + 8 * odd, 4)
            backward(k - 1, shot, 4 + 4 * odd, 4)
            when_late(lambda: leave(shot, late_side, late_id))
        return carry

    lax.fori_loop(0, 4, backward_round, 0)

    per_plane = shots // PLANES
    block_rows = ROWS // per_plane
    cells_all = size * PLANES * ROWS * LANES

    def cut(i, carry):
        blocks[pl.ds(i * per_plane, per_plane)] = (grad[2 + i] / cs[2 + i]).reshape(per_plane, block_rows, LANES)
        return carry

    lax.fori_loop(0, PLANES, cut, 0)

    def remote(source, target, sem, device):
        return pltpu.make_async_remote_copy(
            source, target, all_send.at[sem], all_recv.at[sem], device_id=device, device_id_type=MESH
        )

    def to_shots(source_of, target, sem):
        def one(r):
            j = lax.rem(s + r, shots)
            remote(source_of(j), target, sem, (j, d)).start()

        each(shots, one)

    others, others_depth = pl.ds(0, shots - 1), pl.ds(0, size - 1)
    pl.semaphore_wait(token, rows_y)
    to_shots(lambda j: blocks.at[j], parts.at[s], 0)
    parts[s] = blocks[s]
    remote(parts.at[others], parts.at[others], 0, (s, d)).wait_recv()
    total = lax.fori_loop(1, shots, lambda j, t: t + parts[j], parts[0])
    plane = d * PLANES + s // per_plane
    weight = 1.0 + 2.0 * plane.astype(jnp.float32) / (size * PLANES - 1)
    mine = weight * total
    scaled[s] = mine
    old = moment[s]
    squares = jnp.sum(mine * mine)
    for q, value in enumerate((squares, weight * jnp.sum(old * old), weight * jnp.sum(old * mine), weight * squares)):
        tiles[s, q : q + 1, :] = jnp.full((1, LANES), value, jnp.float32)
    tiles[s, 4:8, :] = jnp.zeros((4, LANES), jnp.float32)
    to_shots(lambda j: tiles.at[s], tiles.at[s], 1)
    to_shots(lambda j: scaled.at[s], scaled.at[s], 2)
    remote(tiles.at[others], tiles.at[others], 1, (s, d)).wait_recv()
    depth_tiles[d] = lax.fori_loop(1, shots, lambda j, t: t + tiles[j], tiles[0])

    def to_depth(r):
        j = lax.rem(d + r, size)
        remote(depth_tiles.at[d], depth_tiles.at[d], 3, (s, j)).start()

    each(size, to_depth)
    remote(depth_tiles.at[others_depth], depth_tiles.at[others_depth], 3, (s, d)).wait_recv()
    grand = lax.fori_loop(1, size, lambda j, t: t + depth_tiles[j], depth_tiles[0])
    step = 0.5 * lax.rsqrt(grand[0:1, :] / cells_all + EPSILON)
    energy = grand[1:2, :] - 2.0 * step * grand[2:3, :] + step * step * grand[3:4, :]
    kinetic_out[...] = 0.5 * energy / cells_all
    remote(scaled.at[others], scaled.at[others], 2, (s, d)).wait_recv()

    def update(j, carry):
        half_out[j] = moment[j] - step * scaled[j]
        return carry

    lax.fori_loop(0, shots, update, 0)

    def sent(side, target):
        for i in range(5):
            parcel_copy(i, side, target).wait_send()
        for shot in range(SHOTS):
            first_copy(shot, side, target).wait_send()
            for slot, buf, level in ((0, u, 2), (1, u, 4), (2, u, 6), (3, u, 8), (4, p, 6), (5, p, 4), (6, p, 2)):
                halo_copy(buf, level, slot, shot, side, 4, target).wait_send()

    sent(early_side, early_id)
    when_late(lambda: sent(late_side, late_id))

    @pl.when(relays)
    def _():
        for i in range(5):
            parcel_from_relay(i, early_side).wait_send()

    remote(parts.at[others], parts.at[others], 0, (s, d)).wait_send()
    remote(tiles.at[others], tiles.at[others], 1, (s, d)).wait_send()
    remote(scaled.at[others], scaled.at[others], 2, (s, d)).wait_send()
    remote(depth_tiles.at[others_depth], depth_tiles.at[others_depth], 3, (s, d)).wait_send()


def window(c, momentum, fprev, fcur, anext, acur, observed, src, rec, ckpt, ns, nd):
    any_space = pl.BlockSpec(memory_space=pl.ANY)
    in_vmem = pl.BlockSpec(memory_space=pltpu.VMEM)
    in_smem = pl.BlockSpec(memory_space=pltpu.SMEM)
    padded = (10, SHOTS, PLANES + 2 * HALO, ROWS + 2 * PAD, LANES)
    f32 = jnp.float32
    blocks = (ns, PLANES * ROWS // ns, LANES)
    half, kinetic = pl.pallas_call(
        window_kernel,
        out_shape=(jax.ShapeDtypeStruct(blocks, f32), jax.ShapeDtypeStruct((1, LANES), f32)),
        in_specs=[any_space] * 5 + [in_vmem, in_smem, in_vmem, in_smem, in_vmem],
        out_specs=(in_vmem, in_vmem),
        scratch_shapes=[
            pltpu.VMEM(padded, f32),
            pltpu.VMEM(padded, f32),
            pltpu.VMEM((STEPS, SHOTS, EXT, ROWS, LANES), f32),
            pltpu.VMEM((STEPS, SHOTS, EXT, ROWS, LANES), f32),
            pltpu.VMEM((SHOTS, EXT, ROWS, LANES), f32),
            pltpu.VMEM((SHOTS, EXT, ROWS, LANES), f32),
            pltpu.VMEM((EXT, ROWS, LANES), f32),
            pltpu.VMEM((EXT, ROWS, LANES), f32),
            pltpu.VMEM((STEPS, LANES), f32),
            pltpu.VMEM((SHOTS, PLANES, ROWS, LANES), f32),
            pltpu.VMEM((SHOTS, PLANES, ROWS, LANES), f32),
            pltpu.VMEM(blocks, f32),
            pltpu.VMEM(blocks, f32),
            pltpu.VMEM(blocks, f32),
            pltpu.VMEM((ns, 8, LANES), f32),
            pltpu.VMEM((nd, 8, LANES), f32),
            pltpu.VMEM((14, ROWS, LANES), f32),
            pltpu.SemaphoreType.DMA((5,)),
            pltpu.SemaphoreType.DMA((7, SHOTS, 2)),
            pltpu.SemaphoreType.DMA((7, SHOTS, 2)),
            pltpu.SemaphoreType.DMA((SHOTS, 2)),
            pltpu.SemaphoreType.DMA((SHOTS, 2)),
            pltpu.SemaphoreType.DMA((5, 2)),
            pltpu.SemaphoreType.DMA((5, 2)),
            pltpu.SemaphoreType.DMA((5,)),
            pltpu.SemaphoreType.DMA((5,)),
            pltpu.SemaphoreType.DMA((4,)),
            pltpu.SemaphoreType.DMA((4,)),
            pltpu.SemaphoreType.REGULAR,
        ],
        compiler_params=pltpu.CompilerParams(
            collective_id=0, has_side_effects=True, vmem_limit_bytes=60 * 1024 * 1024
        ),
        name="window",
    )(c, fprev, fcur, anext, acur, observed, src, rec, ckpt, momentum.reshape(blocks))
    return half.reshape(momentum.shape), kinetic[0, 0]


def solution(mesh):
    def shards(c, momentum, fprev, fcur, anext, acur, observed, src, rec, ckpt):
        return window(
            c, momentum, fprev, fcur, anext, acur, observed, src, rec, ckpt.reshape(1),
            mesh.shape["shot"], mesh.shape["depth"],
        )

    placed = (
        P("depth", None, None),
        P("depth", None, None),
        P("shot", "depth", None, None),
        P("shot", "depth", None, None),
        P("shot", "depth", None, None),
        P("shot", "depth", None, None),
        P("shot", None, None),
        P("shot"),
        P("shot", None),
        P(),
    )
    return jax.shard_map(
        shards, mesh=mesh, in_specs=placed, out_specs=(P("depth", None, None), P()), check_vma=False
    )
```

time: 126 us -> 122 us (0.968)
  Pallas kernels: 122 us -> 118 us
    pallas_call x2 -> x1, Pallas kernels: 122 us -> 118 us  [window(): pl.pallas_call(window_kernel, out_shape=(jax.ShapeDtypeStruct(blocks, f32...]
where the time goes in v2:
time: 122 us
  Pallas kernels  118 us (97%)
  between operations  2.46 us (2%)
  local copies, waits for them, and re-layouts  1.68 us (1%)
    pallas_call x1, Pallas kernels, window(): pl.pallas_call(window_kernel, out_shape=(jax.ShapeDtypeStruct(blocks, f32...  118 us

profile of v2, /device:TPU:1, one launch (start us, length us, event | category | flops | bytes accessed | tf_op | source)
XLA Modules:
  0.0 121.8 jit_solution(15175145190155785848)
XLA Ops:
  1.3 117.6 %window.1 = (f32[32,16,128]{2,1,0:T(8,128)}, f32[1,128]{1,0:T(1,128)}) custom-call(f32[8,64,128]{2,1,0:T(8,128)} %c_in.1, f32[2,8,64,128]{3,2,1,0:T(8,128)} %fprev.1, f32[2,8,64,128]{3,2,1,0:T(8,128)} %fcur.1, f32[2,8,64,128]{3,2,1,0:T(8,128)} %anext.1, f32[2,8,64,128]{3,2,1,0:T(8,128)} %acur.1, f32[2,8,512]{2,1,0:T(8,128)} %observed.1, s32[2]{0:T(128)} %src.1, ...), custom_call_target="tpu_custom_call" | custom-call | tf_op jit(solution)/shard_map/window/pallas_call | solution.py:462
  118.9 0.0 copy-start
  118.9 1.7 %copy.15 = f32[8,64,128]{2,1,0:T(8,128)} copy(f32[8,64,128]{2,1,0:T(8,128)} %bitcast.7) | data formatting | bytes 524288
  120.6 0.0 copy-done
Async XLA Ops:
  118.9 1.7 %copy-start = (f32[1,128]{1,0:T(1,128)S(1)}, f32[1,128]{1,0:T(1,128)}, u32[]{:S(2)}) copy-start(f32[1,128]{1,0:T(1,128)} %get-tuple-element.5) | copy-start | bytes 1540

commit v3 on v2

--- a/solution.py
+++ b/solution.py
@@ -25,11 +25,11 @@
 
 
 def window_kernel(
-    c_in, fprev, fcur, anext, acur, observed, src, rec, ckpt, moment,
+    c_in, fprev, fcur, anext, acur, observed_in, src, rec_in, ckpt, moment_in,
     half_out, kinetic_out,
     u, p, lap, obs, cnt, hot, cs, grad, wave, stage_next, stage_cur,
-    blocks, parts, scaled, tiles, depth_tiles,
-    relay,
+    blocks, parts, scaled, z_tiles, xy_tiles,
+    relay, observed, rec, moment,
     local_sem, send_sem, recv_sem, init_send, init_recv, parcel_send, parcel_recv, relay_send, relay_recv,
     all_send, all_recv, token,
 ):
@@ -37,19 +37,17 @@
     d = lax.axis_index("depth")
     shots, size = lax.axis_size("shot"), lax.axis_size("depth")
     rows_y, half = shots // Z_LO, size // 2
-    y, z_lo, x_core = s // Z_LO, lax.rem(s, Z_LO), lax.rem(d, half)
+    y, z_lo, z_hi, x_core = s // Z_LO, lax.rem(s, Z_LO), d // half, lax.rem(d, half)
+    chips_x, chips_z = half // 2, 2 * Z_LO
+    x, z = x_core // 2, z_hi * Z_LO + z_lo
     odd = lax.rem(d, 2)
     early_side, late_side = 1 - odd, odd
     early_id = (s, d + 1 - 2 * odd)
     has_late = ((odd == 1) & (d < size - 1)) | ((odd == 0) & (d > 0))
     late_id = (s, jnp.clip(d - 1 + 2 * odd, 0, size - 1))
 
-    def each(count, action):
-        def one(r, carry):
-            action(r)
-            return carry
-
-        lax.fori_loop(1, count, one, 0)
+    def outward(count):
+        return sorted(range(count), key=lambda r: -min(r, count - r))
 
     def y_peer(r):
         return (lax.rem(y + r, rows_y) * Z_LO + z_lo, d)
@@ -67,9 +65,12 @@
         greet((s, size - 1 - d))
 
     greet(far_side)
-    each(rows_y, lambda r: greet(y_peer(r)))
-    each(Z_LO, lambda r: greet((y * Z_LO + lax.rem(z_lo + r, Z_LO), d)))
-    each(half, lambda r: greet((s, d - x_core + lax.rem(x_core + r, half))))
+    for r in outward(rows_y)[:-1]:
+        greet(y_peer(r))
+    for r in range(1, Z_LO):
+        greet((y * Z_LO + lax.rem(z_lo + r, Z_LO), d))
+    for r in outward(half)[:-1]:
+        greet((s, d - x_core + lax.rem(x_core + r, half)))
 
     data = pl.ds(PAD, ROWS)
     own = pl.ds(HALO, PLANES)
@@ -79,6 +80,9 @@
         pltpu.make_async_copy(c_in, cs.at[pl.ds(2, PLANES)], local_sem.at[2]),
         pltpu.make_async_copy(acur, stage_cur, local_sem.at[3]),
         pltpu.make_async_copy(anext, stage_next, local_sem.at[4]),
+        pltpu.make_async_copy(observed_in, observed, local_sem.at[5]),
+        pltpu.make_async_copy(rec_in, rec, local_sem.at[6]),
+        pltpu.make_async_copy(moment_in, moment, local_sem.at[7]),
     ]
     for copy in loads:
         copy.start()
@@ -160,7 +164,8 @@
     def pass_on(device):
         pl.semaphore_signal(token, inc=1, device_id=device, device_id_type=MESH)
 
-    each(rows_y, lambda r: pass_on(y_peer(r)))
+    for r in outward(rows_y)[:-1]:
+        pass_on(y_peer(r))
     pass_on(far_side)
 
     loads[2].wait()
@@ -235,13 +240,13 @@
             high = trace.astype(jnp.bfloat16).astype(jnp.float32)
             total = put(high) + put(trace - high)
             obs[k, shot] = total.reshape(EXT, ROWS, LANES)
+        return carry
+
+    cell_at = lax.broadcasted_iota(jnp.int32, (ROWS, LANES), 0) * LANES + lax.broadcasted_iota(jnp.int32, (ROWS, LANES), 1)
+    for shot in range(SHOTS):
         source = src[shot] - first_cell
-        inside = lax.broadcasted_iota(jnp.int32, (ROWS, LANES), 0) * LANES + lax.broadcasted_iota(jnp.int32, (ROWS, LANES), 1)
         for plane in range(EXT):
-            hot[shot, plane] = jnp.where(inside == source - plane * (ROWS * LANES), 1.0, 0.0)
-        return carry
-
-    lax.fori_loop(0, SHOTS, place, 0)
+            hot[shot, plane] = jnp.where(cell_at == source - plane * (ROWS * LANES), 1.0, 0.0)
 
     lane_iota = lax.broadcasted_iota(jnp.int32, (ROWS, LANES), 1)
     masks = {j: (lane_iota >= j) if j > 0 else (lane_iota < LANES + j) for j in (1, 2, -1, -2)}
@@ -303,6 +308,10 @@
         forward(0, shot, 4 + 6 * odd, 2)
         when_late(lambda: halo_copy(u, 2, 0, shot, late_side, 4, late_id).start())
 
+    for load in loads[5:]:
+        load.wait()
+    lax.fori_loop(0, SHOTS, place, 0)
+
     @pl.when(relays)
     def _():
         for i in range(5):
@@ -343,6 +352,24 @@
         parcel_copy(i, 1 - early_side, early_id).wait_recv()
         when_late(lambda: parcel_copy(i, 1 - late_side, late_id).wait_recv())
 
+    per_plane = shots // PLANES
+    block_rows = ROWS // per_plane
+    cells_all = size * PLANES * ROWS * LANES
+
+    def remote(source, target, sem, device):
+        return pltpu.make_async_remote_copy(
+            source, target, all_send.at[sem], all_recv.at[sem], device_id=device, device_id_type=MESH
+        )
+
+    def scatter(side):
+        first = (PLANES // 2) * side
+        for i in range(PLANES // 2):
+            blocks[pl.ds((first + i) * per_plane, per_plane)] = (grad[2 + first + i] / cs[2 + first + i]).reshape(
+                per_plane, block_rows, LANES
+            )
+
+    pl.semaphore_wait(token, rows_y)
+
     def backward_round(i, carry):
         k = 7 - 2 * i
 
@@ -361,6 +388,7 @@
             backward(k, shot, 2 + 4 * even, 8)
             backward(k - 1, shot, 4 + 4 * even, 4)
             leave(shot, early_side, early_id)
+
         for shot in range(SHOTS):
             when_late(lambda: arrive(shot, late_side, late_id))
             backward(k, shot, 2 + 8 * odd, 4)
@@ -370,31 +398,18 @@
 
     lax.fori_loop(0, 4, backward_round, 0)
 
-    per_plane = shots // PLANES
-    block_rows = ROWS // per_plane
-    cells_all = size * PLANES * ROWS * LANES
-
-    def cut(i, carry):
-        blocks[pl.ds(i * per_plane, per_plane)] = (grad[2 + i] / cs[2 + i]).reshape(per_plane, block_rows, LANES)
-        return carry
-
-    lax.fori_loop(0, PLANES, cut, 0)
-
-    def remote(source, target, sem, device):
-        return pltpu.make_async_remote_copy(
-            source, target, all_send.at[sem], all_recv.at[sem], device_id=device, device_id_type=MESH
-        )
-
-    def to_shots(source_of, target, sem):
-        def one(r):
-            j = lax.rem(s + r, shots)
-            remote(source_of(j), target, sem, (j, d)).start()
-
-        each(shots, one)
-
-    others, others_depth = pl.ds(0, shots - 1), pl.ds(0, size - 1)
-    pl.semaphore_wait(token, rows_y)
-    to_shots(lambda j: blocks.at[j], parts.at[s], 0)
+    scatter(late_side)
+    scatter(early_side)
+
+    def shot_peers():
+        for dy in outward(rows_y):
+            for dz in range(Z_LO):
+                if dy or dz:
+                    yield lax.rem(y + dy, rows_y) * Z_LO + lax.rem(z_lo + dz, Z_LO)
+
+    others = pl.ds(0, shots - 1)
+    for j in shot_peers():
+        remote(blocks.at[j], parts.at[s], 0, (j, d)).start()
     parts[s] = blocks[s]
     remote(parts.at[others], parts.at[others], 0, (s, d)).wait_recv()
     total = lax.fori_loop(1, shots, lambda j, t: t + parts[j], parts[0])
@@ -404,31 +419,28 @@
     scaled[s] = mine
     old = moment[s]
     squares = jnp.sum(mine * mine)
+
+    column, plane_at = z * 2 + lax.rem(d, 2), y * chips_x + x
     for q, value in enumerate((squares, weight * jnp.sum(old * old), weight * jnp.sum(old * mine), weight * squares)):
-        tiles[s, q : q + 1, :] = jnp.full((1, LANES), value, jnp.float32)
-    tiles[s, 4:8, :] = jnp.zeros((4, LANES), jnp.float32)
-    to_shots(lambda j: tiles.at[s], tiles.at[s], 1)
-    to_shots(lambda j: scaled.at[s], scaled.at[s], 2)
-    remote(tiles.at[others], tiles.at[others], 1, (s, d)).wait_recv()
-    depth_tiles[d] = lax.fori_loop(1, shots, lambda j, t: t + tiles[j], tiles[0])
-
-    def to_depth(r):
-        j = lax.rem(d + r, size)
-        remote(depth_tiles.at[d], depth_tiles.at[d], 3, (s, j)).start()
-
-    each(size, to_depth)
-    remote(depth_tiles.at[others_depth], depth_tiles.at[others_depth], 3, (s, d)).wait_recv()
-    grand = lax.fori_loop(1, size, lambda j, t: t + depth_tiles[j], depth_tiles[0])
-    step = 0.5 * lax.rsqrt(grand[0:1, :] / cells_all + EPSILON)
-    energy = grand[1:2, :] - 2.0 * step * grand[2:3, :] + step * step * grand[3:4, :]
-    kinetic_out[...] = 0.5 * energy / cells_all
-    remote(scaled.at[others], scaled.at[others], 2, (s, d)).wait_recv()
-
-    def update(j, carry):
-        half_out[j] = moment[j] - step * scaled[j]
-        return carry
-
-    lax.fori_loop(0, shots, update, 0)
+        z_tiles[column, q : q + 1, :] = jnp.full((1, LANES), value, jnp.float32)
+    z_tiles[column, 4:8, :] = jnp.zeros((4, LANES), jnp.float32)
+    for dz in outward(chips_z):
+        to_z = lax.rem(z + dz, chips_z)
+        for flip in range(2):
+            if dz or flip:
+                core = lax.rem(d + flip, 2)
+                device = (y * Z_LO + lax.rem(to_z, Z_LO), (to_z // Z_LO) * half + x * 2 + core)
+                remote(z_tiles.at[column], z_tiles.at[column], 1, device).start()
+    for j in shot_peers():
+        remote(scaled.at[s], scaled.at[s], 2, (j, d)).start()
+    others_z, others_xy = pl.ds(0, 2 * chips_z - 1), pl.ds(0, rows_y * chips_x - 1)
+    remote(z_tiles.at[others_z], z_tiles.at[others_z], 1, (s, d)).wait_recv()
+    xy_tiles[plane_at] = lax.fori_loop(1, 2 * chips_z, lambda j, t: t + z_tiles[j], z_tiles[0])
+    for dy in outward(rows_y):
+        for dx in outward(chips_x):
+            if dy or dx:
+                device = (lax.rem(y + dy, rows_y) * Z_LO + z_lo, z_hi * half + lax.rem(x + dx, chips_x) * 2 + lax.rem(d, 2))
+                remote(xy_tiles.at[plane_at], xy_tiles.at[plane_at], 3, device).start()
 
     def sent(side, target):
         for i in range(5):
@@ -447,9 +459,21 @@
             parcel_from_relay(i, early_side).wait_send()
 
     remote(parts.at[others], parts.at[others], 0, (s, d)).wait_send()
-    remote(tiles.at[others], tiles.at[others], 1, (s, d)).wait_send()
+    remote(z_tiles.at[others_z], z_tiles.at[others_z], 1, (s, d)).wait_send()
     remote(scaled.at[others], scaled.at[others], 2, (s, d)).wait_send()
-    remote(depth_tiles.at[others_depth], depth_tiles.at[others_depth], 3, (s, d)).wait_send()
+    remote(xy_tiles.at[others_xy], xy_tiles.at[others_xy], 3, (s, d)).wait_send()
+    remote(xy_tiles.at[others_xy], xy_tiles.at[others_xy], 3, (s, d)).wait_recv()
+    grand = lax.fori_loop(1, rows_y * chips_x, lambda j, t: t + xy_tiles[j], xy_tiles[0])
+    step = 0.5 * lax.rsqrt(grand[0:1, :] / cells_all + EPSILON)
+    energy = grand[1:2, :] - 2.0 * step * grand[2:3, :] + step * step * grand[3:4, :]
+    kinetic_out[...] = 0.5 * energy / cells_all
+    remote(scaled.at[others], scaled.at[others], 2, (s, d)).wait_recv()
+
+    def update(j, carry):
+        half_out[j] = moment[j] - step * scaled[j]
+        return carry
+
+    lax.fori_loop(0, shots, update, 0)
 
 
 def window(c, momentum, fprev, fcur, anext, acur, observed, src, rec, ckpt, ns, nd):
@@ -462,7 +486,7 @@
     half, kinetic = pl.pallas_call(
         window_kernel,
         out_shape=(jax.ShapeDtypeStruct(blocks, f32), jax.ShapeDtypeStruct((1, LANES), f32)),
-        in_specs=[any_space] * 5 + [in_vmem, in_smem, in_vmem, in_smem, in_vmem],
+        in_specs=[any_space] * 6 + [in_smem, any_space, in_smem, any_space],
         out_specs=(in_vmem, in_vmem),
         scratch_shapes=[
             pltpu.VMEM(padded, f32),
@@ -479,10 +503,13 @@
             pltpu.VMEM(blocks, f32),
             pltpu.VMEM(blocks, f32),
             pltpu.VMEM(blocks, f32),
-            pltpu.VMEM((ns, 8, LANES), f32),
-            pltpu.VMEM((nd, 8, LANES), f32),
+            pltpu.VMEM((4 * Z_LO, 8, LANES), f32),
+            pltpu.VMEM((ns // Z_LO * nd // 4, 8, LANES), f32),
             pltpu.VMEM((14, ROWS, LANES), f32),
-            pltpu.SemaphoreType.DMA((5,)),
+            pltpu.VMEM((SHOTS, STEPS, NREC), f32),
+            pltpu.VMEM((SHOTS, NREC), jnp.int32),
+            pltpu.VMEM(blocks, f32),
+            pltpu.SemaphoreType.DMA((8,)),
             pltpu.SemaphoreType.DMA((7, SHOTS, 2)),
             pltpu.SemaphoreType.DMA((7, SHOTS, 2)),
             pltpu.SemaphoreType.DMA((SHOTS, 2)),

time: 122 us -> 114 us (0.934)
  Pallas kernels: 118 us -> 110 us
    pallas_call x1, Pallas kernels: 118 us -> 110 us  [window(): pl.pallas_call(window_kernel, out_shape=(jax.ShapeDtypeStruct(blocks, f32...]
where the time goes in v3:
time: 114 us
  Pallas kernels  110 us (96%)
  between operations  2.46 us (2%)
  local copies, waits for them, and re-layouts  1.68 us (1%)
    pallas_call x1, Pallas kernels, window(): pl.pallas_call(window_kernel, out_shape=(jax.ShapeDtypeStruct(blocks, f32...  110 us

profile of v3, /device:TPU:1, one launch (start us, length us, event | category | flops | bytes accessed | tf_op | source)
XLA Modules:
  0.0 113.8 jit_solution(3718972783696573131)
XLA Ops:
  1.3 109.7 %window.1 = (f32[32,16,128]{2,1,0:T(8,128)}, f32[1,128]{1,0:T(1,128)}) custom-call(f32[8,64,128]{2,1,0:T(8,128)} %c_in.1, f32[2,8,64,128]{3,2,1,0:T(8,128)} %fprev.1, f32[2,8,64,128]{3,2,1,0:T(8,128)} %fcur.1, f32[2,8,64,128]{3,2,1,0:T(8,128)} %anext.1, f32[2,8,64,128]{3,2,1,0:T(8,128)} %acur.1, f32[2,8,512]{2,1,0:T(8,128)} %observed_in.1, s32[2]{0:T(128)} %src.1, ...), custom_call_target="tpu_custom_call" | custom-call | tf_op jit(solution)/shard_map/window/pallas_call | solution.py:486
  110.9 0.0 copy-start
  111.0 1.7 %copy.15 = f32[8,64,128]{2,1,0:T(8,128)} copy(f32[8,64,128]{2,1,0:T(8,128)} %bitcast.7) | data formatting | bytes 524288
  112.6 0.0 copy-done
Async XLA Ops:
  110.9 1.7 %copy-start = (f32[1,128]{1,0:T(1,128)S(1)}, f32[1,128]{1,0:T(1,128)}, u32[]{:S(2)}) copy-start(f32[1,128]{1,0:T(1,128)} %get-tuple-element.5) | copy-start | bytes 1540

commit v4 on v3

--- a/solution.py
+++ b/solution.py
@@ -29,7 +29,7 @@
     half_out, kinetic_out,
     u, p, lap, obs, cnt, hot, cs, grad, wave, stage_next, stage_cur,
     blocks, parts, scaled, z_tiles, xy_tiles,
-    relay, observed, rec, moment,
+    relay, observed, rec, moment, lines, line_parts,
     local_sem, send_sem, recv_sem, init_send, init_recv, parcel_send, parcel_recv, relay_send, relay_recv,
     all_send, all_recv, token,
 ):
@@ -408,15 +408,40 @@
                     yield lax.rem(y + dy, rows_y) * Z_LO + lax.rem(z_lo + dz, Z_LO)
 
     others = pl.ds(0, shots - 1)
-    for j in shot_peers():
-        remote(blocks.at[j], parts.at[s], 0, (j, d)).start()
-    parts[s] = blocks[s]
-    remote(parts.at[others], parts.at[others], 0, (s, d)).wait_recv()
-    total = lax.fori_loop(1, shots, lambda j, t: t + parts[j], parts[0])
     plane = d * PLANES + s // per_plane
     weight = 1.0 + 2.0 * plane.astype(jnp.float32) / (size * PLANES - 1)
-    mine = weight * total
-    scaled[s] = mine
+    off_cut = jnp.logical_not(at_cut)
+    line = pl.ds(y * Z_LO, Z_LO)
+    others_y, others_line = pl.ds(0, (rows_y - 1) * Z_LO), pl.ds(0, Z_LO - 1)
+
+    def z_peers():
+        for r in range(1, Z_LO):
+            to = lax.rem(z_lo + r, Z_LO)
+            yield to, (y * Z_LO + to, d)
+
+    @pl.when(at_cut)
+    def _():
+        for j in shot_peers():
+            remote(blocks.at[j], parts.at[s], 0, (j, d)).start()
+        parts[s] = blocks[s]
+        remote(parts.at[others], parts.at[others], 0, (s, d)).wait_recv()
+        scaled[s] = weight * lax.fori_loop(1, shots, lambda j, t: t + parts[j], parts[0])
+
+    @pl.when(off_cut)
+    def _():
+        for r in outward(rows_y)[:-1]:
+            to = lax.rem(y + r, rows_y)
+            remote(blocks.at[pl.ds(to * Z_LO, Z_LO)], parts.at[line], 4, y_peer(r)).start()
+        parts[line] = blocks[line]
+        remote(parts.at[others_y], parts.at[others_y], 4, (s, d)).wait_recv()
+        lines[...] = lax.fori_loop(1, rows_y, lambda j, t: t + parts[pl.ds(j * Z_LO, Z_LO)], parts[0:Z_LO])
+        for to, device in z_peers():
+            remote(lines.at[to], line_parts.at[z_lo], 5, device).start()
+        line_parts[z_lo] = lines[z_lo]
+        remote(line_parts.at[others_line], line_parts.at[others_line], 5, (s, d)).wait_recv()
+        scaled[s] = weight * lax.fori_loop(1, Z_LO, lambda j, t: t + line_parts[j], line_parts[0])
+
+    mine = scaled[s]
     old = moment[s]
     squares = jnp.sum(mine * mine)
 
@@ -431,8 +456,20 @@
                 core = lax.rem(d + flip, 2)
                 device = (y * Z_LO + lax.rem(to_z, Z_LO), (to_z // Z_LO) * half + x * 2 + core)
                 remote(z_tiles.at[column], z_tiles.at[column], 1, device).start()
-    for j in shot_peers():
-        remote(scaled.at[s], scaled.at[s], 2, (j, d)).start()
+
+    @pl.when(at_cut)
+    def _():
+        for j in shot_peers():
+            remote(scaled.at[s], scaled.at[s], 2, (j, d)).start()
+
+    @pl.when(off_cut)
+    def _():
+        for _, device in z_peers():
+            remote(scaled.at[s], scaled.at[s], 6, device).start()
+        remote(scaled.at[others_line], scaled.at[others_line], 6, (s, d)).wait_recv()
+        for r in outward(rows_y)[:-1]:
+            remote(scaled.at[line], scaled.at[line], 2, y_peer(r)).start()
+
     others_z, others_xy = pl.ds(0, 2 * chips_z - 1), pl.ds(0, rows_y * chips_x - 1)
     remote(z_tiles.at[others_z], z_tiles.at[others_z], 1, (s, d)).wait_recv()
     xy_tiles[plane_at] = lax.fori_loop(1, 2 * chips_z, lambda j, t: t + z_tiles[j], z_tiles[0])
@@ -458,16 +495,33 @@
         for i in range(5):
             parcel_from_relay(i, early_side).wait_send()
 
-    remote(parts.at[others], parts.at[others], 0, (s, d)).wait_send()
+    @pl.when(at_cut)
+    def _():
+        remote(parts.at[others], parts.at[others], 0, (s, d)).wait_send()
+        remote(scaled.at[others], scaled.at[others], 2, (s, d)).wait_send()
+
+    @pl.when(off_cut)
+    def _():
+        remote(parts.at[others_y], parts.at[others_y], 4, (s, d)).wait_send()
+        remote(line_parts.at[others_line], line_parts.at[others_line], 5, (s, d)).wait_send()
+        remote(scaled.at[others_line], scaled.at[others_line], 6, (s, d)).wait_send()
+        remote(scaled.at[others_y], scaled.at[others_y], 2, (s, d)).wait_send()
+
     remote(z_tiles.at[others_z], z_tiles.at[others_z], 1, (s, d)).wait_send()
-    remote(scaled.at[others], scaled.at[others], 2, (s, d)).wait_send()
     remote(xy_tiles.at[others_xy], xy_tiles.at[others_xy], 3, (s, d)).wait_send()
     remote(xy_tiles.at[others_xy], xy_tiles.at[others_xy], 3, (s, d)).wait_recv()
     grand = lax.fori_loop(1, rows_y * chips_x, lambda j, t: t + xy_tiles[j], xy_tiles[0])
     step = 0.5 * lax.rsqrt(grand[0:1, :] / cells_all + EPSILON)
     energy = grand[1:2, :] - 2.0 * step * grand[2:3, :] + step * step * grand[3:4, :]
     kinetic_out[...] = 0.5 * energy / cells_all
-    remote(scaled.at[others], scaled.at[others], 2, (s, d)).wait_recv()
+
+    @pl.when(at_cut)
+    def _():
+        remote(scaled.at[others], scaled.at[others], 2, (s, d)).wait_recv()
+
+    @pl.when(off_cut)
+    def _():
+        remote(scaled.at[others_y], scaled.at[others_y], 2, (s, d)).wait_recv()
 
     def update(j, carry):
         half_out[j] = moment[j] - step * scaled[j]
@@ -509,6 +563,8 @@
             pltpu.VMEM((SHOTS, STEPS, NREC), f32),
             pltpu.VMEM((SHOTS, NREC), jnp.int32),
             pltpu.VMEM(blocks, f32),
+            pltpu.VMEM((Z_LO,) + blocks[1:], f32),
+            pltpu.VMEM((Z_LO,) + blocks[1:], f32),
             pltpu.SemaphoreType.DMA((8,)),
             pltpu.SemaphoreType.DMA((7, SHOTS, 2)),
             pltpu.SemaphoreType.DMA((7, SHOTS, 2)),
@@ -518,8 +574,8 @@
             pltpu.SemaphoreType.DMA((5, 2)),
             pltpu.SemaphoreType.DMA((5,)),
             pltpu.SemaphoreType.DMA((5,)),
-            pltpu.SemaphoreType.DMA((4,)),
-            pltpu.SemaphoreType.DMA((4,)),
+            pltpu.SemaphoreType.DMA((7,)),
+            pltpu.SemaphoreType.DMA((7,)),
             pltpu.SemaphoreType.REGULAR,
         ],
         compiler_params=pltpu.CompilerParams(

time: 114 us -> 112 us (0.982)
  Pallas kernels: 110 us -> 108 us
    pallas_call x1, Pallas kernels: 110 us -> 108 us  [window(): pl.pallas_call(window_kernel, out_shape=(jax.ShapeDtypeStruct(blocks, f32...]
where the time goes in v4:
time: 112 us
  Pallas kernels  108 us (96%)
  between operations  2.46 us (2%)
  local copies, waits for them, and re-layouts  1.68 us (2%)
    pallas_call x1, Pallas kernels, window(): pl.pallas_call(window_kernel, out_shape=(jax.ShapeDtypeStruct(blocks, f32...  108 us

profile of v4, /device:TPU:1, one launch (start us, length us, event | category | flops | bytes accessed | tf_op | source)
XLA Modules:
  0.0 112.2 jit_solution(10253345529319557974)
XLA Ops:
  1.3 108.1 %window.1 = (f32[32,16,128]{2,1,0:T(8,128)}, f32[1,128]{1,0:T(1,128)}) custom-call(f32[8,64,128]{2,1,0:T(8,128)} %c_in.1, f32[2,8,64,128]{3,2,1,0:T(8,128)} %fprev.1, f32[2,8,64,128]{3,2,1,0:T(8,128)} %fcur.1, f32[2,8,64,128]{3,2,1,0:T(8,128)} %anext.1, f32[2,8,64,128]{3,2,1,0:T(8,128)} %acur.1, f32[2,8,512]{2,1,0:T(8,128)} %observed_in.1, s32[2]{0:T(128)} %src.1, ...), custom_call_target="tpu_custom_call" | custom-call | tf_op jit(solution)/shard_map/window/pallas_call | solution.py:540
  109.4 0.0 copy-start
  109.4 1.7 %copy.15 = f32[8,64,128]{2,1,0:T(8,128)} copy(f32[8,64,128]{2,1,0:T(8,128)} %bitcast.7) | data formatting | bytes 524288
  111.0 0.0 copy-done
Async XLA Ops:
  109.4 1.7 %copy-start = (f32[1,128]{1,0:T(1,128)S(1)}, f32[1,128]{1,0:T(1,128)}, u32[]{:S(2)}) copy-start(f32[1,128]{1,0:T(1,128)} %get-tuple-element.5) | copy-start | bytes 1540

commit v5 on v4

--- a/solution.py
+++ b/solution.py
@@ -299,6 +299,12 @@
     def arrived(buf, level, slot, shot, side, width, target):
         halo_copy(buf, level, slot, shot, 1 - side, width, target).wait_recv()
 
+    @pl.when(relays)
+    def _():
+        for i in range(5):
+            parcel_to_relay(i, early_side).wait_recv()
+            parcel_from_relay(i, early_side).start()
+
     for shot in range(SHOTS):
         first_copy(shot, 1 - early_side, early_id).wait_recv()
         forward(0, shot, 4 + 2 * even, 6)
@@ -311,12 +317,6 @@
     for load in loads[5:]:
         load.wait()
     lax.fori_loop(0, SHOTS, place, 0)
-
-    @pl.when(relays)
-    def _():
-        for i in range(5):
-            parcel_to_relay(i, early_side).wait_recv()
-            parcel_from_relay(i, early_side).start()
 
     parcel_copy(0, 1 - early_side, early_id).wait_recv()
     when_late(lambda: parcel_copy(0, 1 - late_side, late_id).wait_recv())

time: 112 us -> 111 us (level)
    pallas_call x1, Pallas kernels: 108 us -> 107 us  [window(): pl.pallas_call(window_kernel, out_shape=(jax.ShapeDtypeStruct(blocks, f32...]
where the time goes in v5:
time: 111 us
  Pallas kernels  107 us (96%)
  between operations  2.46 us (2%)
  local copies, waits for them, and re-layouts  1.68 us (2%)
    pallas_call x1, Pallas kernels, window(): pl.pallas_call(window_kernel, out_shape=(jax.ShapeDtypeStruct(blocks, f32...  107 us

profile of v5, /device:TPU:1, one launch (start us, length us, event | category | flops | bytes accessed | tf_op | source)
XLA Modules:
  0.0 110.9 jit_solution(9871538875791531770)
XLA Ops:
  1.3 106.8 %window.1 = (f32[32,16,128]{2,1,0:T(8,128)}, f32[1,128]{1,0:T(1,128)}) custom-call(f32[8,64,128]{2,1,0:T(8,128)} %c_in.1, f32[2,8,64,128]{3,2,1,0:T(8,128)} %fprev.1, f32[2,8,64,128]{3,2,1,0:T(8,128)} %fcur.1, f32[2,8,64,128]{3,2,1,0:T(8,128)} %anext.1, f32[2,8,64,128]{3,2,1,0:T(8,128)} %acur.1, f32[2,8,512]{2,1,0:T(8,128)} %observed_in.1, s32[2]{0:T(128)} %src.1, ...), custom_call_target="tpu_custom_call" | custom-call | tf_op jit(solution)/shard_map/window/pallas_call | solution.py:540
  108.1 0.0 copy-start
  108.1 1.7 %copy.15 = f32[8,64,128]{2,1,0:T(8,128)} copy(f32[8,64,128]{2,1,0:T(8,128)} %bitcast.7) | data formatting | bytes 524288
  109.7 0.0 copy-done
Async XLA Ops:
  108.1 1.7 %copy-start = (f32[1,128]{1,0:T(1,128)S(1)}, f32[1,128]{1,0:T(1,128)}, u32[]{:S(2)}) copy-start(f32[1,128]{1,0:T(1,128)} %get-tuple-element.5) | copy-start | bytes 1540
